TPU v7x, 32 devices: a whole 2x2x4 slice. The times are simulated.
32 devices in a mesh: dp: 4 (over x, core), expert: 8 (over z, y).
Axes of the slice: x: 2, y: 2, z: 4, core: 2. Of those that a mesh axis runs over, the one named last changes fastest.
Arguments:
- tokens_in: bfloat16 [4096, 2048], P(('dp', 'expert')), may hold values from -6 to 6
- out_grad: bfloat16 [4096, 2048], P(('dp', 'expert')), may hold values from -6 to 6
- gate_logits: float32 [4096, 8], P(('dp', 'expert')), may hold values from -6 to 6
- route_ids: int32 [4096, 8], P(('dp', 'expert')), may hold values from 0 to 15, all different within a row; in each aligned block of 128 rows (0 to 127, 128 to 255, ...) at most 72 rows name the same one
- w_gate: bfloat16 [2048, 16, 768], P(None, 'expert'), may hold values from -0.125 to 0.125
- w_up: bfloat16 [2048, 16, 768], P(None, 'expert'), may hold values from -0.125 to 0.125
- w_down: bfloat16 [2048, 16, 768], P(None, 'expert'), may hold values from -0.21875 to 0.21875
Outputs:
- input_grad: bfloat16 [4096, 2048], P(('dp', 'expert'))
- router_grad: float32 [4096, 8], P(('dp', 'expert'))
- weight_grads: bfloat16 [2048, 3, 16, 768], P('dp', None, 'expert')
Inputs may be any that keep to these rules, and one draw needn't show every extreme that they name: `route_ids`: the 8 experts of a token differ. In each aligned block of 128 rows (the rows of one device) no expert is named by more than 72 rows, a bound that some block reaches.
All inputs are finite; a program needn't handle non-finite values.
Results may differ from a plain program's by a relative error of at most 0.015.
Values may be sent and summed in bfloat16 or wider, within the bound.
A program may use at most 192 MiB of HBM per device.

v0:
```python
import jax
import jax.numpy as jnp
from jax import lax
from jax.sharding import PartitionSpec as P


def combine_weights(gate_logits):
    raised = jnp.exp(gate_logits)
    return raised / jnp.sum(raised, axis=1, keepdims=True)


def rounded(term):
    return lax.optimization_barrier(term.astype(jnp.bfloat16)).astype(jnp.float32)


def per_device(tokens_in, out_grad, gate_logits, route_ids, w_gate, w_up, w_down):
    tok_rows, model_width = tokens_in.shape
    topk_count = route_ids.shape[1]
    local_experts = w_gate.shape[1]
    owners = lax.axis_size("expert")
    expert_count = local_experts * owners
    capacity = 9 * tok_rows * topk_count // (8 * expert_count)
    pair_count = tok_rows * topk_count
    slot_count = expert_count * capacity
    weights = combine_weights(gate_logits)
    scaled = (weights[:, :, None] * out_grad[:, None, :].astype(jnp.float32)).astype(jnp.bfloat16)
    flat_ids = route_ids.reshape(-1)
    onehot = (flat_ids[:, None] == jnp.arange(expert_count, dtype=jnp.int32)[None, :]).astype(
        jnp.int32
    )
    before = jnp.cumsum(onehot, axis=0) - onehot
    slot_rank = jnp.sum(before * onehot, axis=1)
    slot_of_pair = flat_ids * capacity + slot_rank
    pair_of_slot = (
        jnp.full((slot_count,), pair_count, jnp.int32)
        .at[slot_of_pair]
        .set(jnp.arange(pair_count, dtype=jnp.int32))
    )
    zero_row = jnp.zeros((1, model_width), jnp.bfloat16)
    token_table = jnp.concatenate([tokens_in, zero_row], axis=0)
    scaled_table = jnp.concatenate([scaled.reshape(pair_count, model_width), zero_row], axis=0)
    send_shape = (owners, local_experts * capacity, model_width)
    send_tokens = jnp.take(token_table, pair_of_slot // topk_count, axis=0).reshape(send_shape)
    send_scaled = jnp.take(scaled_table, pair_of_slot, axis=0).reshape(send_shape)
    recv_tokens, recv_scaled = (
        lax.all_to_all(send_tokens, "expert", split_axis=0, concat_axis=0, tiled=True),
        lax.all_to_all(send_scaled, "expert", split_axis=0, concat_axis=0, tiled=True),
    )
    block_shape = (owners, local_experts, capacity, model_width)
    recv_tokens = recv_tokens.reshape(block_shape)
    recv_scaled = recv_scaled.reshape(block_shape)
    gate_pre = jnp.einsum("nemd,deh->nemh", recv_tokens, w_gate, preferred_element_type=jnp.float32)
    up_pre = jnp.einsum("nemd,deh->nemh", recv_tokens, w_up, preferred_element_type=jnp.float32)
    sigmoid_gate = jax.nn.sigmoid(gate_pre)
    active = gate_pre * sigmoid_gate
    hidden = (active * up_pre).astype(jnp.bfloat16)
    hidden_grad = jnp.einsum(
        "nemd,deh->nemh", recv_scaled, w_down, preferred_element_type=jnp.float32
    )
    prob_part = jnp.sum(hidden_grad * hidden.astype(jnp.float32), axis=3).astype(jnp.bfloat16)
    gate_grad = (
        hidden_grad * up_pre * sigmoid_gate * (1.0 + gate_pre * (1.0 - sigmoid_gate))
    ).astype(jnp.bfloat16)
    up_grad = (hidden_grad * active).astype(jnp.bfloat16)
    row_grad = (
        jnp.einsum("nemh,deh->nemd", gate_grad, w_gate, preferred_element_type=jnp.float32)
        + jnp.einsum("nemh,deh->nemd", up_grad, w_up, preferred_element_type=jnp.float32)
    ).astype(jnp.bfloat16)
    back_rows, back_probs = (
        lax.all_to_all(
            row_grad.reshape(send_shape), "expert", split_axis=0, concat_axis=0, tiled=True
        ),
        lax.all_to_all(
            prob_part.reshape(owners, local_experts * capacity),
            "expert",
            split_axis=0,
            concat_axis=0,
            tiled=True,
        ),
    )
    pair_rows = jnp.take(back_rows.reshape(slot_count, model_width), slot_of_pair, axis=0)
    input_grad = jnp.sum(
        pair_rows.reshape(tok_rows, topk_count, model_width).astype(jnp.float32), axis=1
    ).astype(jnp.bfloat16)
    pair_probs = (
        jnp.take(back_probs.reshape(slot_count), slot_of_pair, axis=0)
        .reshape(tok_rows, topk_count)
        .astype(jnp.float32)
    )
    router_grad = pair_probs - weights * jnp.sum(pair_probs, axis=1, keepdims=True)
    grad_gate = jnp.einsum(
        "nemd,nemh->deh", recv_tokens, gate_grad, preferred_element_type=jnp.float32
    )
    grad_up = jnp.einsum("nemd,nemh->deh", recv_tokens, up_grad, preferred_element_type=jnp.float32)
    grad_down = jnp.einsum(
        "nemd,nemh->deh", recv_scaled, hidden, preferred_element_type=jnp.float32
    )
    shares = lax.psum_scatter(
        rounded(jnp.stack([grad_gate, grad_up, grad_down], axis=1)).astype(jnp.bfloat16),
        "dp",
        scatter_dimension=0,
        tiled=True,
    )
    return (input_grad, router_grad, shares)


def solution(mesh):
    in_specs = (
        P(("dp", "expert"), None),
        P(("dp", "expert"), None),
        P(("dp", "expert"), None),
        P(("dp", "expert"), None),
        P(None, "expert", None),
        P(None, "expert", None),
        P(None, "expert", None),
    )
    out_specs = (
        P(("dp", "expert"), None),
        P(("dp", "expert"), None),
        P("dp", None, "expert", None),
    )
    return jax.shard_map(
        per_device, mesh=mesh, in_specs=in_specs, out_specs=out_specs, check_vma=False
    )
```

profile of v0, /device:TPU:0, one launch (start us, length us, event | category | flops | bytes accessed | tf_op | source)
XLA Modules:
  0.0 472.4 jit_solution(5095138765060391296)
XLA Ops:
  7.2 0.8 copy.59
  8.0 0.1 eq.26
  8.1 0.1 reshape.135
  8.1 0.1 mul.76
  8.3 4.5 reduce-window.6
  12.9 0.1 copy.62
  13.3 4.3 scatter_custom_fusion
  17.6 0.1 broadcast_in_dim.58
  17.7 1.1 concatenate.7
  18.8 5.9 %gather_fusion.1 = bf16[1152,2048]{1,0:T(8,128)(2,1)} fusion(bf16[129,2048]{1,0:T(8,128)(2,1)S(1)} %concatenate.7, s32[2048]{0:T(1024)S(1)} %pad_clamp_fusion), kind=kCustom, calls=%fused_computation.1 | custom fusion | bytes 9441792 | tf_op jit(solution)/shard_map/jit(_take)/gather | solution.py:43
  24.7 5.0 %broadcast_select_fusion = bf16[8,144,2048]{2,1,0:T(8,128)(2,1)} fusion(bf16[8,144,2048]{2,1,0:T(8,128)(2,1)} %bitcast.117, pred[8,144]{1,0:T(8,128)(4,1)S(1)} %broadcast_in_dim.58), kind=kLoop, calls=%fused_computation.26 | loop fusion | flops 2359296 | bytes 9438336 | tf_op jit(solution)/shard_map/jit(_take)/select_n | solution.py:43
  29.7 7.4 %all-to-all-start.1 = ((bf16[8,144,2048]{2,1,0:T(8,128)(2,1)}), bf16[8,144,2048]{2,1,0:T(8,128)(2,1)}, u32[]{:S(2)}, u32[]{:S(2)}) async-start(bf16[8,144,2048]{2,1,0:T(8,128)(2,1)} %broadcast_select_fusion), calls=%async_computation.1 | async-start | bytes 9437184 | tf_op jit(solution)/shard_map/all_to_all | solution.py:46
  37.2 0.1 convert_element_type.57
  37.3 0.1 copy.64
  37.4 0.1 exponential_reduce_fusion
  37.5 0.1 exponential_divide_fusion
  37.6 0.1 mul.77
  37.7 0.9 fusion
  38.6 2.4 concatenate.6
  41.0 0.1 broadcast_in_dim.54
  41.1 13.5 %gather_fusion = bf16[1152,2048]{1,0:T(8,128)(2,1)} fusion(bf16[1025,2048]{1,0:T(8,128)(2,1)} %concatenate.6, s32[2048]{0:T(1024)S(1)} %pad_clamp_fusion.1), kind=kCustom, calls=%fused_computation | custom fusion | bytes 9441792 | tf_op jit(solution)/shard_map/jit(_take)/gather | solution.py:44
  54.6 5.1 %broadcast_select_fusion.1 = bf16[8,144,2048]{2,1,0:T(8,128)(2,1)} fusion(bf16[8,144,2048]{2,1,0:T(8,128)(2,1)} %bitcast.118, pred[8,144]{1,0:T(8,128)(4,1)S(1)} %broadcast_in_dim.54), kind=kLoop, calls=%fused_computation.27 | loop fusion | flops 2359296 | bytes 9438336 | tf_op jit(solution)/shard_map/jit(_take)/select_n | solution.py:44
  59.7 82.0 %all-to-all-done.1 = bf16[8,144,2048]{2,1,0:T(8,128)(2,1)} async-done(((bf16[8,144,2048]{2,1,0:T(8,128)(2,1)}), bf16[8,144,2048]{2,1,0:T(8,128)(2,1)}, u32[]{:S(2)}, u32[]{:S(2)}) %all-to-all-start.1) | async-done | bytes 4718624 | tf_op jit(solution)/shard_map/all_to_all | solution.py:46
  141.7 4.6 all-to-all-start
  146.3 0.2 reduce-scatter.2.cloned.1.call-start
  146.5 9.8 %fusion.12 = f32[2,8,72,768]{3,2,1,0:T(8,128)} fusion(bf16[2048,2,768,1]{2,1,0,3:T(2,128)(2,1)} %bitcast.127, bf16[8,2,72,2048]{3,2,1,0:T(8,128)(2,1)} %bitcast.10), kind=kOutput, calls=%fused_computation.23 | convolution fusion | flops 3623878656 | bytes 14548992 | tf_op jit(solution)/shard_map/nemd,deh->nemh/dot_general | solution.py:53
  156.4 9.8 %fusion.8 = f32[2,8,72,768]{3,2,1,0:T(8,128)} fusion(bf16[2048,2,768,1]{2,1,0,3:T(2,128)(2,1)} %bitcast.125, bf16[8,2,72,2048]{3,2,1,0:T(8,128)(2,1)} %bitcast.10), kind=kOutput, calls=%fused_computation.19 | convolution fusion | flops 3623878656 | bytes 14548992 | tf_op jit(solution)/shard_map/nemd,deh->nemh/dot_general | solution.py:52
  166.2 83.9 %all-to-all-done = bf16[8,144,2048]{2,1,0:T(8,128)(2,1)} async-done(((bf16[8,144,2048]{2,1,0:T(8,128)(2,1)}), bf16[8,144,2048]{2,1,0:T(8,128)(2,1)}, u32[]{:S(2)}, u32[]{:S(2)}) %all-to-all-start) | async-done | bytes 4718624 | tf_op jit(solution)/shard_map/all_to_all | solution.py:47
  250.0 11.1 %fusion.29 = (bf16[8,2,72]{2,0,1:T(8,128)(2,1)S(1)}, bf16[8,2,72,768]{3,2,0,1:T(8,128)(2,1)S(1)}, bf16[8,2,72,768]{3,2,0,1:T(8,128)(2,1)S(1)}, bf16[8,2,72,768]{3,2,0,1:T(8,128)(2,1)S(1)}) fusion(f32[2,8,72,768]{3,2,1,0:T(8,128)} %fusion.12, f32[2,8,72,768]{3,2,1,0:T(8,128)} %fusion.8, bf16[2048,2,768,1]{2,1,0,3:T(2,128)(2,1)} %bitcast.124, ...), kind=kOutput, calls=%fused_computation.48 | convolution fusion | flops 3639802880 | bytes 23398656 | tf_op jit(solution)/shard_map/nemd,deh->nemh/dot_general | solution.py:57
  261.1 8.3 %fusion.3 = bf16[2048,1,2,768]{0,3,2,1:T(8,128)(2,1)S(1)} fusion(bf16[8,2,72,768]{3,2,0,1:T(8,128)(2,1)S(1)} %get-tuple-element.18, bf16[8,2,72,2048]{3,2,1,0:T(8,128)(2,1)} %bitcast.6), kind=kOutput, calls=%fused_computation.14 | convolution fusion | flops 3627024384 | bytes 12779520 | tf_op jit(solution)/shard_map/nemd,nemh->deh/dot_general | solution.py:95
  269.5 7.7 %fusion.2 = bf16[2048,1,2,768]{0,3,2,1:T(8,128)(2,1)S(1)} fusion(bf16[8,2,72,768]{3,2,0,1:T(8,128)(2,1)S(1)} %get-tuple-element.22, bf16[8,2,72,2048]{3,2,1,0:T(8,128)(2,1)} %bitcast.10), kind=kOutput, calls=%fused_computation.13 | convolution fusion | flops 3627024384 | bytes 12779520 | tf_op jit(solution)/shard_map/nemd,nemh->deh/dot_general | solution.py:94
  277.2 7.7 %fusion.1 = bf16[2048,1,2,768]{0,3,2,1:T(8,128)(2,1)S(1)} fusion(bf16[8,2,72,768]{3,2,0,1:T(8,128)(2,1)S(1)} %get-tuple-element.21, bf16[8,2,72,2048]{3,2,1,0:T(8,128)(2,1)} %bitcast.10), kind=kOutput, calls=%fused_computation.12 | convolution fusion | flops 3627024384 | bytes 12779520 | tf_op jit(solution)/shard_map/nemd,nemh->deh/dot_general | solution.py:91
  284.9 8.3 %pad_maximum_fusion = bf16[2048,3,2,768]{0,3,2,1:T(8,128)(2,1)} fusion(bf16[2048,1,2,768]{0,3,2,1:T(8,128)(2,1)S(1)} %fusion.3, bf16[2048,1,2,768]{0,3,2,1:T(8,128)(2,1)S(1)} %fusion.2, bf16[2048,1,2,768]{0,3,2,1:T(8,128)(2,1)S(1)} %fusion.1), kind=kLoop, calls=%fused_computation.5 | loop fusion | flops 18874368 | bytes 37748736 | tf_op jit(solution)/shard_map/stack | solution.py:99
  293.3 0.7 convert_element_type.68
  294.0 3.9 all-to-all-start.3
  297.9 13.9 %fusion.6 = f32[2,8,72,2048]{3,2,1,0:T(8,128)} fusion(bf16[8,2,72,768]{3,2,0,1:T(8,128)(2,1)} %copy-done.2, bf16[2048,2,768,1]{2,1,0,3:T(2,128)(2,1)} %bitcast.126), kind=kOutput, calls=%fused_computation.17 | convolution fusion | flops 3623878656 | bytes 17498112 | tf_op jit(solution)/shard_map/nemh,deh->nemd/dot_general | solution.py:66
  311.8 11.0 %fusion.14 = bf16[8,2,72,2048]{3,2,0,1:T(8,128)(2,1)S(1)} fusion(f32[2,8,72,2048]{3,2,1,0:T(8,128)} %fusion.6, bf16[8,2,72,768]{3,2,0,1:T(8,128)(2,1)S(1)} %get-tuple-element.22, bf16[2048,2,768,1]{2,1,0,3:T(2,128)(2,1)} %bitcast.128), kind=kOutput, calls=%fused_computation.25 | convolution fusion | flops 3628597248 | bytes 22216704 | tf_op jit(solution)/shard_map/nemh,deh->nemd/dot_general | solution.py:67
  322.8 2.8 copy.73
  325.6 6.0 %all-to-all-start.2 = ((bf16[8,144,2048]{2,1,0:T(8,128)(2,1)}), bf16[8,144,2048]{2,1,0:T(8,128)(2,1)}, u32[]{:S(2)}, u32[]{:S(2)}) async-start(bf16[8,144,2048]{2,1,0:T(8,128)(2,1)} %bitcast.116), calls=%async_computation.2 | async-start | bytes 9437184 | tf_op jit(solution)/shard_map/all_to_all | solution.py:70
  331.7 0.1 reshape.141
  331.8 6.8 %gather_fusion.3 = bf16[1024]{0:T(1024)(128)(2,1)S(1)} fusion(bf16[1152]{0:T(1024)(128)(2,1)S(1)} %reshape.141, s32[1024]{0:T(1024)S(1)} %broadcast_clamp_fusion), kind=kCustom, calls=%fused_computation.3 | custom fusion | bytes 8192 | tf_op jit(solution)/shard_map/jit(_take)/gather | solution.py:86
  338.7 0.1 convert_reduce_fusion
  338.8 0.1 convert_subtract_fusion
  338.9 0.7 copy.79
  339.6 96.2 %all-to-all-done.2 = bf16[8,144,2048]{2,1,0:T(8,128)(2,1)} async-done(((bf16[8,144,2048]{2,1,0:T(8,128)(2,1)}), bf16[8,144,2048]{2,1,0:T(8,128)(2,1)}, u32[]{:S(2)}, u32[]{:S(2)}) %all-to-all-start.2) | async-done | bytes 4718624 | tf_op jit(solution)/shard_map/all_to_all | solution.py:70
  435.8 11.8 %gather_fusion.2 = bf16[1024,2048]{1,0:T(8,128)(2,1)} fusion(bf16[1152,2048]{1,0:T(8,128)(2,1)} %bitcast.19, s32[1024]{0:T(1024)S(1)} %broadcast_clamp_fusion), kind=kCustom, calls=%fused_computation.2 | custom fusion | bytes 8392704 | tf_op jit(solution)/shard_map/jit(_take)/gather | solution.py:81
  447.6 5.1 %fusion.15 = bf16[128,2048]{1,0:T(8,128)(2,1)} fusion(bf16[1024,2048]{1,0:T(8,128)(2,1)} %gather_fusion.2, pred[128,8]{1,0:T(8,128)(4,1)S(1)} %get-tuple-element.16), kind=kLoop, calls=%fused_computation.29 | loop fusion | flops 3932160 | bytes 4719616 | tf_op jit(solution)/shard_map/reduce_sum | solution.py:82
  452.7 12.4 %copy.80 = bf16[512,3,2,768]{3,2,1,0:T(2,128)(2,1)} copy(bf16[512,3,2,768]{0,3,2,1:T(8,128)(2,1)} %reduce-scatter.2.cloned.1.call-done) | data formatting | bytes 9437184
  (28 shorter events, 0.6 us)
Async XLA Ops:
  29.7 7.4 %copy-start = (bf16[128,2048]{1,0:T(8,128)(2,1)S(1)}, bf16[128,2048]{1,0:T(8,128)(2,1)}, u32[]{:S(2)}) copy-start(bf16[128,2048]{1,0:T(8,128)(2,1)} %param.8) | copy-start | bytes 1572868
  29.7 7.5 %copy-start.1 = (f32[128,8]{0,1:T(8,128)S(1)}, f32[128,8]{0,1:T(8,128)}, u32[]{:S(2)}) copy-start(f32[128,8]{0,1:T(8,128)} %param.9) | copy-start | bytes 12292
  29.7 111.9 %all-to-all-start.1 = ((bf16[8,144,2048]{2,1,0:T(8,128)(2,1)}), bf16[8,144,2048]{2,1,0:T(8,128)(2,1)}, u32[]{:S(2)}, u32[]{:S(2)}) async-start(bf16[8,144,2048]{2,1,0:T(8,128)(2,1)} %broadcast_select_fusion), calls=%async_computation.1 | async-start | bytes 9437184 | tf_op jit(solution)/shard_map/all_to_all | solution.py:46
  141.7 108.4 %all-to-all-start = ((bf16[8,144,2048]{2,1,0:T(8,128)(2,1)}), bf16[8,144,2048]{2,1,0:T(8,128)(2,1)}, u32[]{:S(2)}, u32[]{:S(2)}) async-start(bf16[8,144,2048]{2,1,0:T(8,128)(2,1)} %broadcast_select_fusion.1), calls=%async_computation | async-start | bytes 9437184 | tf_op jit(solution)/shard_map/all_to_all | solution.py:47
  146.3 306.4 %reduce-scatter.2.cloned.1.call-start = ((), (), s32[]{:S(2)}) async-start(), calls=%async_computation.5 | async-start | bytes 23592960 | tf_op jit(solution)/shard_map/reduce_scatter | solution.py:98
  261.1 16.1 %copy-start.2 = (bf16[8,2,72,768]{3,2,0,1:T(8,128)(2,1)}, bf16[8,2,72,768]{3,2,0,1:T(8,128)(2,1)S(1)}, u32[]{:S(2)}) copy-start(bf16[8,2,72,768]{3,2,0,1:T(8,128)(2,1)S(1)} %get-tuple-element.21) | copy-start | bytes 5308420
  294.0 31.6 %all-to-all-start.3 = ((bf16[8,1,144]{2,1,0:T(2,128)(2,1)}), bf16[8,1,144]{2,1,0:T(2,128)(2,1)S(1)}, u32[]{:S(2)}, u32[]{:S(2)}) async-start(bf16[8,1,144]{2,1,0:T(2,128)(2,1)} %convert_element_type.68), calls=%async_computation.3 | async-start | bytes 16384 | tf_op jit(solution)/shard_map/all_to_all | solution.py:73
  325.6 110.2 %all-to-all-start.2 = ((bf16[8,144,2048]{2,1,0:T(8,128)(2,1)}), bf16[8,144,2048]{2,1,0:T(8,128)(2,1)}, u32[]{:S(2)}, u32[]{:S(2)}) async-start(bf16[8,144,2048]{2,1,0:T(8,128)(2,1)} %bitcast.116), calls=%async_computation.2 | async-start | bytes 9437184 | tf_op jit(solution)/shard_map/all_to_all | solution.py:70
Sparse Core Ops, SparseCore 0:
  293.4 138.4 reduce-scatter.1
where the time goes:
time: 479 us; the launch traced here: 472 us
  waiting for transfers between devices  262 us (55%)
  matrix products  79.4 us (17%)
  local copies, waits for them, and re-layouts  64.3 us (13%)
  other arithmetic  29.8 us (6%)
  starting transfers between devices  22.1 us (5%)
  between operations  14.7 us (3%)
    all_to_all x1, waiting for transfers between devices, per_device(): lax.all_to_all(row_grad.reshape(send_shape), 'expert', split_axis=0, conc...  96.2 us
    all_to_all x1, waiting for transfers between devices, per_device(): lax.all_to_all(send_scaled, 'expert', split_axis=0, concat_axis=0, tiled=...  83.9 us
    all_to_all x1, waiting for transfers between devices, per_device(): lax.all_to_all(send_tokens, 'expert', split_axis=0, concat_axis=0, tiled=...  82 us
    unnamed x10, local copies, waits for them, and re-layouts  14 us
    dot_general x1, matrix products, per_device(): jnp.einsum('nemh,deh->nemd', gate_grad, w_gate, preferred_element_type=jn...  13.9 us
    gather x1, local copies, waits for them, and re-layouts, per_device(): jnp.take(scaled_table, pair_of_slot, axis=0).reshape(send_shape)  13.5 us
    gather x1, local copies, waits for them, and re-layouts, per_device(): jnp.take(back_rows.reshape(slot_count, model_width), slot_of_pair, axis=0)  11.8 us
    dot_general x1, matrix products, per_device(): jnp.einsum('nemd,deh->nemh', recv_scaled, w_down, preferred_element_type=...  11.1 us
  transfers between devices with their start and end apart: 5, of which 3 were waited for; matrix products, arithmetic and copies ran while one was open for 20% of the time, Pallas kernels for 0%

commit v1 on v0

v1 whole, which is shorter than its diff:
```python
import jax
import jax.numpy as jnp
from jax import lax
from jax.sharding import PartitionSpec as P

BF16 = jnp.bfloat16
F32 = jnp.float32


def combine_weights(gate_logits):
    raised = jnp.exp(gate_logits)
    return raised / jnp.sum(raised, axis=1, keepdims=True)


def per_device(tokens_in, out_grad, gate_logits, route_ids, w_gate, w_up, w_down):
    tok_rows, model_width = tokens_in.shape
    topk_count = route_ids.shape[1]
    local_experts = w_gate.shape[1]
    hidden_width = w_gate.shape[2]
    owners = lax.axis_size("expert")
    expert_count = local_experts * owners
    capacity = 9 * tok_rows * topk_count // (8 * expert_count)
    row_count = owners * capacity
    weights = combine_weights(gate_logits)

    meta = jnp.concatenate([weights, route_ids.astype(F32)], axis=1)
    meta = lax.all_gather(meta, "expert", axis=0)
    all_tokens = lax.all_gather(tokens_in, "expert", axis=0)
    all_grads = lax.all_gather(out_grad, "expert", axis=0)

    w_gu = lax.optimization_barrier(
        jnp.concatenate([jnp.transpose(w_gate, (1, 0, 2)), jnp.transpose(w_up, (1, 0, 2))], axis=2)
    )
    w_dn = lax.optimization_barrier(jnp.transpose(w_down, (1, 0, 2)))

    all_weights = meta[:, :, :topk_count]
    all_ids = meta[:, :, topk_count:].astype(jnp.int32)
    mine = lax.axis_index("expert") * local_experts + jnp.arange(local_experts, dtype=jnp.int32)
    hit = all_ids[:, None, :, :] == mine[None, :, None, None]
    named = jnp.any(hit, axis=3)
    pair_weight = jnp.sum(jnp.where(hit, all_weights[:, None], 0.0), axis=3)
    earlier = (
        jnp.arange(tok_rows, dtype=jnp.int32)[:, None]
        < jnp.arange(tok_rows, dtype=jnp.int32)[None, :]
    ).astype(BF16)
    rank = jnp.einsum("nes,st->net", named.astype(BF16), earlier, preferred_element_type=F32)
    rank = jnp.where(named, rank.astype(jnp.int32), -1)
    chosen = rank[:, :, None, :] == jnp.arange(capacity, dtype=jnp.int32)[None, None, :, None]
    select = lax.optimization_barrier(chosen.astype(BF16))
    slot_weight = jnp.sum(jnp.where(chosen, pair_weight[:, :, None, :], 0.0), axis=3)

    def dispatch(blocks):
        return jnp.einsum("nect,ntd->necd", select, blocks, preferred_element_type=F32)

    def expert_major(rows):
        return jnp.transpose(rows, (1, 0, 2, 3)).reshape(local_experts, row_count, rows.shape[3])

    rows_in = expert_major(dispatch(all_tokens).astype(BF16))
    pre = jnp.einsum("emd,edh->emh", rows_in, w_gu, preferred_element_type=F32)
    gate_pre, up_pre = pre[:, :, :hidden_width], pre[:, :, hidden_width:]
    sigmoid_gate = jax.nn.sigmoid(gate_pre)
    active = gate_pre * sigmoid_gate
    hidden = (active * up_pre).astype(BF16)

    rows_scaled = expert_major(
        (slot_weight[:, :, :, None] * dispatch(all_grads)).astype(BF16)
    )
    hidden_grad = jnp.einsum("emd,edh->emh", rows_scaled, w_dn, preferred_element_type=F32)
    grad_down = jnp.einsum("emd,emh->edh", rows_scaled, hidden, preferred_element_type=F32)
    share_down = lax.psum_scatter(grad_down.astype(BF16), "dp", scatter_dimension=1, tiled=True)
    prob_part = jnp.sum(hidden_grad * hidden.astype(F32), axis=2).astype(BF16)
    gate_grad = (
        hidden_grad * up_pre * sigmoid_gate * (1.0 + gate_pre * (1.0 - sigmoid_gate))
    ).astype(BF16)
    up_grad = (hidden_grad * active).astype(BF16)
    both_grad = jnp.concatenate([gate_grad, up_grad], axis=2)
    grad_both = jnp.einsum("emd,emh->edh", rows_in, both_grad, preferred_element_type=F32)
    share_both = lax.psum_scatter(grad_both.astype(BF16), "dp", scatter_dimension=1, tiled=True)

    row_grad = jnp.einsum("emh,edh->emd", both_grad, w_gu, preferred_element_type=F32).astype(BF16)
    row_grad = row_grad.reshape(local_experts, owners, capacity, model_width)
    partial = jnp.einsum("nect,encd->ntd", select, row_grad, preferred_element_type=F32)
    input_grad = lax.psum_scatter(
        partial.astype(BF16).reshape(owners * tok_rows, model_width),
        "expert",
        scatter_dimension=0,
        tiled=True,
    )
    slot_prob = prob_part.astype(F32).reshape(local_experts, owners, capacity)
    slot_prob = jnp.transpose(slot_prob, (1, 0, 2))
    token_prob = jnp.sum(jnp.where(chosen, slot_prob[:, :, :, None], 0.0), axis=2)
    probs = jnp.sum(jnp.where(hit, token_prob[:, :, :, None], 0.0), axis=1)
    pair_probs = lax.psum_scatter(
        probs.reshape(owners * tok_rows, topk_count), "expert", scatter_dimension=0, tiled=True
    )
    router_grad = pair_probs - weights * jnp.sum(pair_probs, axis=1, keepdims=True)

    shares = jnp.stack(
        [share_both[:, :, :hidden_width], share_both[:, :, hidden_width:], share_down], axis=0
    )
    return (input_grad, router_grad, jnp.transpose(shares, (2, 0, 1, 3)))


def solution(mesh):
    rows = P(("dp", "expert"), None)
    experts = P(None, "expert", None)
    in_specs = (rows, rows, rows, rows, experts, experts, experts)
    out_specs = (rows, rows, P("dp", None, "expert", None))
    return jax.shard_map(
        per_device, mesh=mesh, in_specs=in_specs, out_specs=out_specs, check_vma=False
    )
```

time: 479 us -> 506 us (1.056); the launches traced: 472 us -> 506 us
  waiting for transfers between devices: 262 us -> 341 us
  local copies, waits for them, and re-layouts: 64.3 us -> 19.6 us
  blocking collectives: 0 us -> 32.5 us
  starting transfers between devices: 22.1 us -> 0.24 us
  matrix products: 79.4 us -> 73 us
    all_to_all x4 -> x0, waiting for transfers between devices: 262 us -> none  [the longest x1 96.2 us: per_device(): lax.all_to_all(row_grad.reshape(send_shape), 'expert', split_axis=0, conc...]
    reduce_scatter x1 -> x4, waiting for transfers between devices: 0.01 us -> 245 us  [the longest x1 98.6 us: per_device(): lax.psum_scatter(grad_both.astype(BF16), 'dp', scatter_dimension=1, tiled...]
    all_gather x0 -> x2, waiting for transfers between devices: none -> 93.9 us  [the longest x1 67.8 us: per_device(): all_tokens = lax.all_gather(tokens_in, 'expert', axis=0)]
    gather x5 -> x0, local copies, waits for them, and re-layouts: 38 us -> none  [the longest x1 13.5 us: per_device(): jnp.take(scaled_table, pair_of_slot, axis=0).reshape(send_shape)]
    all_gather x0 -> x1, blocking collectives: none -> 32.5 us  [per_device(): meta = lax.all_gather(meta, 'expert', axis=0)]
    all_to_all x4 -> x0, starting transfers between devices: 21.9 us -> none  [the longest x1 7.41 us: per_device(): lax.all_to_all(send_tokens, 'expert', split_axis=0, concat_axis=0, tiled=...]
    concatenate x0 -> x2, other arithmetic: none -> 16.3 us  [the longest x1 16.3 us: per_device(): jnp.concatenate([jnp.transpose(w_gate, (1, 0, 2)), jnp.transpose(w_up, (1...]
    another operation x4 -> x0, other arithmetic: 13 us -> none  [the longest x1 8.35 us: per_device(): jnp.stack([grad_gate, grad_up, grad_down], axis=1)]
  transfers between devices with their start and end apart: 5 -> 6, of which waited for: 3 -> 6; matrix products, arithmetic and copies ran while one was open for 20% -> 17% of each run, Pallas kernels for 0% -> 0%
where the time goes in v1:
time: 506 us
  waiting for transfers between devices  341 us (67%)
  matrix products  73 us (14%)
  blocking collectives  32.5 us (6%)
  other arithmetic  25.4 us (5%)
  local copies, waits for them, and re-layouts  19.6 us (4%)
  between operations  14.2 us (3%)
    reduce_scatter x1, waiting for transfers between devices, per_device(): lax.psum_scatter(grad_both.astype(BF16), 'dp', scatter_dimension=1, tiled...  98.6 us
    reduce_scatter x1, waiting for transfers between devices, per_device(): lax.psum_scatter(partial.astype(BF16).reshape(owners * tok_rows, model_wi...  79.5 us
    all_gather x1, waiting for transfers between devices, per_device(): all_tokens = lax.all_gather(tokens_in, 'expert', axis=0)  67.8 us
    reduce_scatter x1, waiting for transfers between devices, per_device(): lax.psum_scatter(grad_down.astype(BF16), 'dp', scatter_dimension=1, tiled...  58.7 us
    all_gather x1, blocking collectives, per_device(): meta = lax.all_gather(meta, 'expert', axis=0)  32.5 us
    all_gather x1, waiting for transfers between devices, per_device(): all_grads = lax.all_gather(out_grad, 'expert', axis=0)  26.2 us
    concatenate x1, other arithmetic, per_device(): jnp.concatenate([jnp.transpose(w_gate, (1, 0, 2)), jnp.transpose(w_up, (1...  16.3 us
    dot_general x1, matrix products, per_device(): jnp.einsum('emd,emh->edh', rows_in, both_grad, preferred_element_type=F32)  15.5 us
  transfers between devices with their start and end apart: 6, of which 6 were waited for; matrix products, arithmetic and copies ran while one was open for 17% of the time, Pallas kernels for 0%

profile of v1, /device:TPU:0, one launch (start us, length us, event | category | flops | bytes accessed | tf_op | source)
XLA Modules:
  0.0 505.9 jit_solution(17685010973492305961)
XLA Ops:
  7.2 0.0 all-gather.6.cloned.1.call-start
  7.2 0.7 all-gather.6.cloned.1.call-update
  7.9 0.0 all-gather.8.cloned.1.call-start
  7.9 0.7 all-gather.8.cloned.1.call-update
  8.6 0.0 reduce-scatter.7.cloned.1.call-start
  8.7 0.7 convert_element_type.59
  9.4 0.7 exponential_reduce_fusion
  10.1 0.7 exponential_divide_fusion
  10.8 32.5 %all-gather = f32[1024,16]{0,1:T(8,128)S(1)} all-gather(f32[128,16]{0,1:T(8,128)S(1)} %pad_maximum_fusion.4), channel_id=2, replica_groups=mesh['dp'=4,'expert'=8] {'expert'}, dimensions={0}, use_global_device_ids=true | all-gather | bytes 73728 | tf_op jit(solution)/shard_map/all_gather | solution.py:27
  43.4 0.1 compare_reduce_fusion
  43.5 0.1 fusion.15
  43.6 0.1 fusion.16
  43.7 16.3 %pad_maximum_fusion = bf16[2,2048,1536]{2,0,1:T(2,128)(2,1)} fusion(bf16[2,2048,768]{2,0,1:T(2,128)(2,1)} %bitcast.59, bf16[2,2048,768]{2,0,1:T(2,128)(2,1)} %bitcast.60), kind=kLoop, calls=%fused_computation | loop fusion | flops 25165824 | bytes 25165824 | tf_op jit(solution)/shard_map/concatenate | solution.py:32
  60.0 0.1 fusion.17
  60.1 0.4 select_reduce_fusion.1
  60.5 26.2 %all-gather.6.cloned.1.call-done = bf16[1024,2048]{1,0:T(8,128)(2,1)} async-done(((bf16[128,2048]{1,0:T(8,128)(2,1)}), bf16[1024,2048]{1,0:T(8,128)(2,1)}) %all-gather.6.cloned.1.call-update) | async-done | bytes 4194320 | tf_op jit(solution)/shard_map/all_gather | solution.py:29
  86.6 3.6 fusion.4
  90.2 2.5 copy.34
  92.7 67.8 %all-gather.8.cloned.1.call-done = bf16[1024,2048]{1,0:T(8,128)(2,1)} async-done(((bf16[128,2048]{1,0:T(8,128)(2,1)}), bf16[1024,2048]{1,0:T(8,128)(2,1)}) %all-gather.8.cloned.1.call-update) | async-done | bytes 4194320 | tf_op jit(solution)/shard_map/all_gather | solution.py:28
  160.5 3.7 convert_bitcast_fusion
  164.2 2.8 copy.36
  167.0 1.3 slice-done.2
  168.3 11.2 %fusion.2 = f32[2,576,1536]{2,1,0:T(8,128)} fusion(bf16[2,576,2048]{2,1,0:T(8,128)(2,1)} %bitcast.63, bf16[2,2048,1536]{2,0,1:T(2,128)(2,1)S(1)} %bitcast.56), kind=kOutput, calls=%fused_computation.3 | convolution fusion | flops 7247757312 | bytes 24379392 | tf_op jit(solution)/shard_map/emd,edh->emh/dot_general | solution.py:59
  179.5 12.7 %multiply_reduce_fusion = (bf16[2,576]{1,0:T(2,128)(2,1)S(1)}, bf16[2,576,768]{2,1,0:T(8,128)(2,1)S(1)}, bf16[2,576,768]{2,1,0:T(8,128)(2,1)}, bf16[2,576,768]{2,1,0:T(8,128)(2,1)}) fusion(f32[2,576,1536]{2,1,0:T(8,128)} %fusion.2, bf16[2,576,2048]{2,1,0:T(8,128)(2,1)} %bitcast.61, bf16[2,2048,768]{2,0,1:T(2,128)(2,1)} %bitcast.71), kind=kOutput, calls=%fused_computation.18 | convolution fusion | flops 3639802880 | bytes 23398656 | tf_op jit(solution)/shard_map/emd,edh->emh/dot_general | solution.py:68
  192.3 0.1 reshape.44
  192.4 0.2 select_reduce_fusion
  192.6 0.7 fusion.18
  193.3 0.0 reduce-scatter.7.cloned.1.call-update
  193.3 0.0 reduce-scatter.9.cloned.1.call-start
  193.3 15.5 %convolution_convert_fusion = bf16[2,2048,1536]{2,1,0:T(8,128)(2,1)} fusion(bf16[2,576,2048]{2,1,0:T(8,128)(2,1)} %bitcast.64, bf16[2,576,768]{2,1,0:T(8,128)(2,1)} %get-tuple-element.14, bf16[2,576,768]{2,1,0:T(8,128)(2,1)} %get-tuple-element.15), kind=kOutput, calls=%fused_computation.5 | convolution fusion | flops 7261126656 | bytes 20840448 | tf_op jit(solution)/shard_map/emd,emh->edh/dot_general | solution.py:77
  208.9 0.0 reduce-scatter.9.cloned.1.call-update
  208.9 0.0 reduce-scatter.11.cloned.1.call-start
  209.0 10.7 %convolution_convert_fusion.1 = bf16[2,2048,768]{2,1,0:T(8,128)(2,1)} fusion(bf16[2,576,2048]{2,1,0:T(8,128)(2,1)} %bitcast.62, bf16[2,576,768]{2,1,0:T(8,128)(2,1)S(1)} %get-tuple-element.13), kind=kOutput, calls=%fused_computation.15 | convolution fusion | flops 3627024384 | bytes 12779520 | tf_op jit(solution)/shard_map/emd,emh->edh/dot_general | solution.py:69
  219.6 0.0 reduce-scatter.11.cloned.1.call-update
  219.6 0.0 reduce-scatter.5.cloned.1.call-start
  219.7 1.4 copy-done.1
  221.1 12.2 %fusion.9 = bf16[2,576,2048]{2,1,0:T(8,128)(2,1)S(1)} fusion(bf16[2,2048,1536]{2,0,1:T(2,128)(2,1)} %pad_maximum_fusion, bf16[2,576,768]{2,1,0:T(8,128)(2,1)S(1)} %copy-done.1, bf16[2,576,768]{2,1,0:T(8,128)(2,1)} %get-tuple-element.15), kind=kOutput, calls=%fused_computation.16 | convolution fusion | flops 7257194496 | bytes 20840448 | tf_op jit(solution)/shard_map/emh,edh->emd/dot_general | solution.py:80
  233.3 3.3 bitcast_convert_fusion
  236.6 0.0 reduce-scatter.5.cloned.1.call-update
  236.6 8.6 %reduce-scatter.7.cloned.1.call-done = f32[128,8]{0,1:T(8,128)} async-done(((f32[1024,8]{0,1:T(8,128)}), f32[128,8]{0,1:T(8,128)}) %reduce-scatter.7.cloned.1.call-update) | async-done | bytes 4112 | tf_op jit(solution)/shard_map/reduce_scatter | solution.py:93
  245.3 0.7 reduce_sum.69
  245.9 1.3 multiply_subtract_fusion
  247.2 98.6 %reduce-scatter.9.cloned.1.call-done = bf16[2,512,1536]{2,1,0:T(8,128)(2,1)} async-done(((bf16[2,2048,1536]{2,1,0:T(8,128)(2,1)}), bf16[2,512,1536]{2,1,0:T(8,128)(2,1)}) %reduce-scatter.9.cloned.1.call-update) | async-done | bytes 3145744 | tf_op jit(solution)/shard_map/reduce_scatter | solution.py:78
  345.8 2.1 slice_bitcast_fusion.1
  347.9 58.7 %reduce-scatter.11.cloned.1.call-done = bf16[2,512,768]{2,1,0:T(8,128)(2,1)} async-done(((bf16[2,2048,768]{2,1,0:T(8,128)(2,1)}), bf16[2,512,768]{2,1,0:T(8,128)(2,1)}) %reduce-scatter.11.cloned.1.call-update) | async-done | bytes 1572880 | tf_op jit(solution)/shard_map/reduce_scatter | solution.py:70
  406.6 3.5 maximum_bitcast_fusion
  410.1 9.4 %copy.41 = bf16[512,3,2,768]{3,2,1,0:T(2,128)(2,1)} copy(bf16[512,3,2,768]{3,0,2,1:T(8,128)(2,1)} %maximum_bitcast_fusion) | data formatting | bytes 9437184
  419.5 79.5 %reduce-scatter.5.cloned.1.call-done = bf16[128,2048]{1,0:T(8,128)(2,1)} async-done(((bf16[1024,2048]{1,0:T(8,128)(2,1)}), bf16[128,2048]{1,0:T(8,128)(2,1)}) %reduce-scatter.5.cloned.1.call-update) | async-done | bytes 524304 | tf_op jit(solution)/shard_map/reduce_scatter | solution.py:83
  (17 shorter events, 0.1 us)
Async XLA Ops:
  7.2 79.5 %all-gather.6.cloned.1.call-start = ((), (), s32[]{:S(2)}) async-start(), calls=%async_computation.8 | async-start | bytes 4718592 | tf_op jit(solution)/shard_map/all_gather | solution.py:29
  7.9 152.6 %all-gather.8.cloned.1.call-start = ((), (), s32[]{:S(2)}) async-start(), calls=%async_computation.9 | async-start | bytes 4718592 | tf_op jit(solution)/shard_map/all_gather | solution.py:28
  8.6 236.6 %reduce-scatter.7.cloned.1.call-start = ((), (), s32[]{:S(2)}) async-start(), calls=%async_computation.5 | async-start | bytes 36864 | tf_op jit(solution)/shard_map/reduce_scatter | solution.py:93
  160.5 6.5 %slice-start = ((s8[12582912]{0:T(1024)(128)(4,1)}), s8[4194304]{0:T(1024)(128)(4,1)S(1)}, s32[]{:S(2)}) async-start(s8[12582912]{0:T(1024)(128)(4,1)} %bitcast.55), calls=%async_computation.10 | async-start | bytes 8388608
  160.5 6.5 %slice-start.1 = ((s8[12582912]{0:T(1024)(128)(4,1)}), s8[4194304]{0:T(1024)(128)(4,1)S(1)}, s32[]{:S(2)}) async-start(s8[12582912]{0:T(1024)(128)(4,1)} %bitcast.55), calls=%async_computation.11 | async-start | bytes 8388608
  164.2 4.1 slice-start.2
  193.3 152.5 %reduce-scatter.9.cloned.1.call-start = ((), (), s32[]{:S(2)}) async-start(), calls=%async_computation.6 | async-start | bytes 15728640 | tf_op jit(solution)/shard_map/reduce_scatter | solution.py:78
  208.9 197.7 %reduce-scatter.11.cloned.1.call-start = ((), (), s32[]{:S(2)}) async-start(), calls=%async_computation.7 | async-start | bytes 7864320 | tf_op jit(solution)/shard_map/reduce_scatter | solution.py:70
  219.6 1.5 copy-start.1
  219.6 279.4 %reduce-scatter.5.cloned.1.call-start = ((), (), s32[]{:S(2)}) async-start(), calls=%async_computation.4 | async-start | bytes 4718592 | tf_op jit(solution)/shard_map/reduce_scatter | solution.py:83
  233.3 12.6 %copy-start = (f32[128,8]{0,1:T(8,128)S(1)}, f32[128,8]{0,1:T(8,128)}, u32[]{:S(2)}) copy-start(f32[128,8]{0,1:T(8,128)} %param.9) | copy-start | bytes 12292
Sparse Core Ops, SparseCore 0:
  10.1 76.4 all-gather.5
  88.8 71.6 all-gather.7
  193.4 51.7 reduce-scatter.6
  247.7 98.0 reduce-scatter.8
  348.2 58.3 reduce-scatter.10
  411.1 87.8 reduce-scatter.4

commit v2 on v1

--- a/solution.py
+++ b/solution.py
@@ -11,6 +11,76 @@
     raised = jnp.exp(gate_logits)
     return raised / jnp.sum(raised, axis=1, keepdims=True)
 
+LINE = 4
+
+
+def add(*terms):
+    total = terms[0].astype(F32)
+    for term in terms[1:]:
+        total = total + term.astype(F32)
+    return total
+
+
+def gather_blocks(block, owners):
+    if owners != 2 * LINE:
+        return lax.all_gather(block, "expert", axis=0)
+    place = lax.axis_index("expert") // 2
+    ups, downs = [block], [block]
+    for step in range(1, LINE):
+        up = [(i, i + 2) for i in range(owners - 2) if i // 2 >= step - 1]
+        down = [(i, i - 2) for i in range(2, owners) if LINE - 1 - i // 2 >= step - 1]
+        ups.append(lax.ppermute(ups[-1], "expert", up))
+        downs.append(lax.ppermute(downs[-1], "expert", down))
+    column = [block]
+    for step in range(1, LINE):
+        column.append(jnp.where(place >= step, ups[step], downs[LINE - step]))
+    swap = [(i, i ^ 1) for i in range(owners)]
+    return jnp.stack(column + [lax.ppermute(one, "expert", swap) for one in column])
+
+
+def scatter_blocks(part_of, owners, dtype):
+    if owners != 2 * LINE:
+        parts = part_of(list(range(owners))).astype(dtype)
+        return lax.psum_scatter(parts, "expert", scatter_dimension=0, tiled=False)
+    swap = [(i, i ^ 1) for i in range(owners)]
+    column = {}
+    for pair in ((1, 3), (2, 0)):
+        there = part_of([LINE + one for one in pair]).astype(dtype)
+        back = lax.ppermute(there, "expert", swap)
+        both = add(part_of(list(pair)), back)
+        column[pair[0]], column[pair[1]] = both[0], both[1]
+    ups, downs = None, None
+    for step in range(1, LINE):
+        up = [(i, i + 2) for i in range(owners - 2) if i // 2 + LINE - step <= LINE - 1]
+        down = [(i, i - 2) for i in range(2, owners) if i // 2 >= LINE - step]
+        send_up = column[step] if ups is None else add(column[step], ups)
+        send_down = column[LINE - step] if downs is None else add(column[LINE - step], downs)
+        ups = lax.ppermute(send_up.astype(dtype), "expert", up)
+        downs = lax.ppermute(send_down.astype(dtype), "expert", down)
+    return add(column[0], ups, downs).astype(dtype)
+
+
+def reduced_product(rows, grads):
+    group = lax.axis_index("dp")
+    chip, core = group // 2, group % 2
+    width = rows.shape[2] // 4
+
+    def product(to_chip, to_core):
+        start = (to_chip * 2 + to_core) * width
+        part = lax.dynamic_slice_in_dim(rows, start, width, axis=2)
+        return jnp.einsum("emd,emh->edh", part, grads, preferred_element_type=F32)
+
+    def over_core(part):
+        return lax.ppermute(part.astype(BF16), "dp", [(0, 1), (1, 0), (2, 3), (3, 2)])
+
+    def over_chip(part):
+        return lax.ppermute(part.astype(BF16), "dp", [(0, 2), (2, 0), (1, 3), (3, 1)])
+
+    far = over_core(product(1 - chip, 1 - core))
+    near = over_core(product(chip, 1 - core))
+    far = over_chip(add(product(1 - chip, core), far))
+    return add(product(chip, core), near, far).astype(BF16)
+
 
 def per_device(tokens_in, out_grad, gate_logits, route_ids, w_gate, w_up, w_down):
     tok_rows, model_width = tokens_in.shape
@@ -23,10 +93,10 @@
     row_count = owners * capacity
     weights = combine_weights(gate_logits)
 
-    meta = jnp.concatenate([weights, route_ids.astype(F32)], axis=1)
-    meta = lax.all_gather(meta, "expert", axis=0)
-    all_tokens = lax.all_gather(tokens_in, "expert", axis=0)
-    all_grads = lax.all_gather(out_grad, "expert", axis=0)
+    meta = jnp.concatenate([weights.T, route_ids.T.astype(F32)], axis=0)
+    meta = jnp.transpose(gather_blocks(meta, owners), (0, 2, 1))
+    all_tokens = gather_blocks(tokens_in, owners)
+    all_grads = gather_blocks(out_grad, owners)
 
     w_gu = lax.optimization_barrier(
         jnp.concatenate([jnp.transpose(w_gate, (1, 0, 2)), jnp.transpose(w_up, (1, 0, 2))], axis=2)
@@ -66,33 +136,32 @@
         (slot_weight[:, :, :, None] * dispatch(all_grads)).astype(BF16)
     )
     hidden_grad = jnp.einsum("emd,edh->emh", rows_scaled, w_dn, preferred_element_type=F32)
-    grad_down = jnp.einsum("emd,emh->edh", rows_scaled, hidden, preferred_element_type=F32)
-    share_down = lax.psum_scatter(grad_down.astype(BF16), "dp", scatter_dimension=1, tiled=True)
+    share_down = reduced_product(rows_scaled, hidden)
     prob_part = jnp.sum(hidden_grad * hidden.astype(F32), axis=2).astype(BF16)
     gate_grad = (
         hidden_grad * up_pre * sigmoid_gate * (1.0 + gate_pre * (1.0 - sigmoid_gate))
     ).astype(BF16)
     up_grad = (hidden_grad * active).astype(BF16)
     both_grad = jnp.concatenate([gate_grad, up_grad], axis=2)
-    grad_both = jnp.einsum("emd,emh->edh", rows_in, both_grad, preferred_element_type=F32)
-    share_both = lax.psum_scatter(grad_both.astype(BF16), "dp", scatter_dimension=1, tiled=True)
+    share_both = reduced_product(rows_in, both_grad)
 
     row_grad = jnp.einsum("emh,edh->emd", both_grad, w_gu, preferred_element_type=F32).astype(BF16)
     row_grad = row_grad.reshape(local_experts, owners, capacity, model_width)
-    partial = jnp.einsum("nect,encd->ntd", select, row_grad, preferred_element_type=F32)
-    input_grad = lax.psum_scatter(
-        partial.astype(BF16).reshape(owners * tok_rows, model_width),
-        "expert",
-        scatter_dimension=0,
-        tiled=True,
-    )
+
+    def partial(slots):
+        kept = jnp.stack([select[one] for one in slots])
+        rows = jnp.stack([row_grad[:, one] for one in slots], axis=1)
+        return jnp.einsum("nect,encd->ntd", kept, rows, preferred_element_type=F32)
+
+    input_grad = scatter_blocks(partial, owners, BF16)
     slot_prob = prob_part.astype(F32).reshape(local_experts, owners, capacity)
     slot_prob = jnp.transpose(slot_prob, (1, 0, 2))
     token_prob = jnp.sum(jnp.where(chosen, slot_prob[:, :, :, None], 0.0), axis=2)
     probs = jnp.sum(jnp.where(hit, token_prob[:, :, :, None], 0.0), axis=1)
-    pair_probs = lax.psum_scatter(
-        probs.reshape(owners * tok_rows, topk_count), "expert", scatter_dimension=0, tiled=True
-    )
+    probs = jnp.transpose(probs, (0, 2, 1))
+    pair_probs = scatter_blocks(
+        lambda slots: jnp.stack([probs[one] for one in slots]), owners, F32
+    ).T
     router_grad = pair_probs - weights * jnp.sum(pair_probs, axis=1, keepdims=True)
 
     shares = jnp.stack(

time: 506 us -> 414 us (0.82); the launches traced: 506 us -> 407 us
  waiting for transfers between devices: 341 us -> 197 us
  starting transfers between devices: 0.24 us -> 77.5 us
  blocking collectives: 32.5 us -> 0 us
  between operations: 14.2 us -> 1.84 us
  other arithmetic: 25.4 us -> 34.8 us
    reduce_scatter x4 -> x0, waiting for transfers between devices: 245 us -> none  [the longest x1 98.6 us: per_device(): lax.psum_scatter(grad_both.astype(BF16), 'dp', scatter_dimension=1, tiled...]
    ppermute x0 -> x52, waiting for transfers between devices: none -> 197 us  [the longest x12 55.5 us: gather_blocks(): lax.ppermute(one, 'expert', swap)]
    all_gather x2 -> x0, waiting for transfers between devices: 93.9 us -> none  [the longest x1 67.8 us: per_device(): all_tokens = lax.all_gather(tokens_in, 'expert', axis=0)]
    ppermute x0 -> x52, starting transfers between devices: none -> 77.5 us  [the longest x6 21.1 us: scatter_blocks(): ups = lax.ppermute(send_up.astype(dtype), 'expert', up)]
    all_gather x1 -> x0, blocking collectives: 32.5 us -> none  [per_device(): meta = lax.all_gather(meta, 'expert', axis=0)]
    convert_element_type x1 -> x6, other arithmetic: 0.69 us -> 7.25 us  [the longest x1 4.19 us: reduced_product(): return add(product(chip, core), near, far).astype(BF16)]
    unnamed x12 -> x53, local copies, waits for them, and re-layouts: 12.1 us -> 18.6 us
    dot_general x3 -> x12, matrix products: 29.5 us -> 33.4 us  [the longest x8 29 us: product(): return jnp.einsum('emd,emh->edh', part, grads, preferred_element_type=F32)]
  transfers between devices with their start and end apart: 6 -> 52, of which waited for: 6 -> 16; matrix products, arithmetic and copies ran while one was open for 17% -> 17% of each run, Pallas kernels for 0% -> 0%
where the time goes in v2:
time: 414 us; the launch traced here: 407 us
  waiting for transfers between devices  197 us (48%)
  starting transfers between devices  77.5 us (19%)
  matrix products  72.9 us (18%)
  other arithmetic  34.8 us (8%)
  local copies, waits for them, and re-layouts  22.7 us (5%)
    ppermute x12, waiting for transfers between devices, gather_blocks(): lax.ppermute(one, 'expert', swap)  55.5 us
    ppermute x2, waiting for transfers between devices, over_chip(): lax.ppermute(part.astype(BF16), 'dp', [(0, 2), (2, 0), (1, 3), (3, 1)])  51.4 us
    ppermute x9, waiting for transfers between devices, gather_blocks(): downs.append(lax.ppermute(downs[-1], 'expert', down))  50.9 us
    dot_general x8, matrix products, product(): return jnp.einsum('emd,emh->edh', part, grads, preferred_element_type=F32)  29 us
    ppermute x4, waiting for transfers between devices, scatter_blocks(): back = lax.ppermute(there, 'expert', swap)  22.5 us
    ppermute x6, starting transfers between devices, scatter_blocks(): ups = lax.ppermute(send_up.astype(dtype), 'expert', up)  21.1 us
    unnamed x53, local copies, waits for them, and re-layouts  18.6 us
    concatenate x1, other arithmetic, per_device(): jnp.concatenate([jnp.transpose(w_gate, (1, 0, 2)), jnp.transpose(w_up, (1...  16.4 us
  transfers between devices with their start and end apart: 52, of which 16 were waited for; matrix products, arithmetic and copies ran while one was open for 17% of the time, Pallas kernels for 0%

profile of v2, /device:TPU:0, one launch (start us, length us, event | category | flops | bytes accessed | tf_op | source)
XLA Modules:
  0.0 406.5 jit_solution(13376868524347599198)
XLA Ops:
  4.0 5.6 %collective-permute-start = (f32[16,128]{1,0:T(8,128)S(1)}, f32[16,128]{1,0:T(8,128)S(1)}, u32[]{:S(2)}, u32[]{:S(2)}) collective-permute-start(f32[16,128]{1,0:T(8,128)S(1)} %pad_maximum_fusion.2), channel_id=1, source_target_pairs={{0,2},{1,3},{2,4},{3,5},{4,6},{5,7},{8,10},{9,11},{10,12},{11,13},... | collective-permute-start | bytes 24584 | tf_op jit(solution)/shard_map/ppermute | solution.py:32
  9.6 2.0 collective-permute-start.6
  11.6 3.5 collective-permute-start.20
  15.7 1.9 bitcast_dynamic-update-slice_fusion.7
  17.6 16.4 %pad_maximum_fusion = bf16[2,2048,1536]{2,0,1:T(2,128)(2,1)} fusion(bf16[2,2048,768]{2,0,1:T(2,128)(2,1)} %bitcast.196, bf16[2,2048,768]{2,0,1:T(2,128)(2,1)} %bitcast.197), kind=kLoop, calls=%fused_computation | loop fusion | flops 25165824 | bytes 25165824 | tf_op jit(solution)/shard_map/concatenate | solution.py:102
  36.8 3.5 collective-permute-done.2
  43.1 3.0 collective-permute-done.3
  46.8 2.2 collective-permute-start.10
  49.0 1.6 collective-permute-start.7
  50.6 2.1 collective-permute-done.7
  54.2 2.1 collective-permute-done.8
  57.9 2.1 collective-permute-done.9
  64.3 16.5 %collective-permute-done.11 = bf16[128,2048]{1,0:T(8,128)(2,1)S(1)} collective-permute-done((bf16[128,2048]{1,0:T(8,128)(2,1)S(1)}, bf16[128,2048]{1,0:T(8,128)(2,1)S(1)}, u32[]{:S(2)}, u32[]{:S(2)}) %collective-permute-start.11) | collective-permute-done | bytes 524320 | tf_op jit(solution)/shard_map/ppermute | solution.py:33
  82.1 9.9 %collective-permute-done.22 = bf16[128,2048]{1,0:T(8,128)(2,1)S(1)} collective-permute-done((bf16[128,2048]{1,0:T(8,128)(2,1)S(1)}, bf16[128,2048]{1,0:T(8,128)(2,1)S(1)}, u32[]{:S(2)}, u32[]{:S(2)}) %collective-permute-start.22) | collective-permute-done | bytes 524320 | tf_op jit(solution)/shard_map/ppermute | solution.py:33
  96.7 4.4 %collective-permute-done.12 = bf16[128,2048]{1,0:T(8,128)(2,1)S(1)} collective-permute-done((bf16[128,2048]{1,0:T(8,128)(2,1)S(1)}, bf16[128,2048]{1,0:T(8,128)(2,1)S(1)}, u32[]{:S(2)}, u32[]{:S(2)}) %collective-permute-start.12) | collective-permute-done | bytes 524320 | tf_op jit(solution)/shard_map/ppermute | solution.py:33
  101.8 8.0 %collective-permute-done.23 = bf16[128,2048]{1,0:T(8,128)(2,1)S(1)} collective-permute-done((bf16[128,2048]{1,0:T(8,128)(2,1)S(1)}, bf16[128,2048]{1,0:T(8,128)(2,1)S(1)}, u32[]{:S(2)}, u32[]{:S(2)}) %collective-permute-start.23) | collective-permute-done | bytes 524320 | tf_op jit(solution)/shard_map/ppermute | solution.py:33
  115.4 5.5 %collective-permute-done.13 = bf16[128,2048]{1,0:T(8,128)(2,1)S(1)} collective-permute-done((bf16[128,2048]{1,0:T(8,128)(2,1)S(1)}, bf16[128,2048]{1,0:T(8,128)(2,1)S(1)}, u32[]{:S(2)}, u32[]{:S(2)}) %collective-permute-start.13) | collective-permute-done | bytes 524320 | tf_op jit(solution)/shard_map/ppermute | solution.py:33
  125.8 25.4 %collective-permute-done.27 = bf16[128,2048]{1,0:T(8,128)(2,1)S(1)} collective-permute-done((bf16[128,2048]{1,0:T(8,128)(2,1)S(1)}, bf16[128,2048]{1,0:T(8,128)(2,1)S(1)}, u32[]{:S(2)}, u32[]{:S(2)}) %collective-permute-start.27) | collective-permute-done | bytes 524320 | tf_op jit(solution)/shard_map/ppermute | solution.py:38
  152.9 23.7 %collective-permute-done.17 = bf16[128,2048]{1,0:T(8,128)(2,1)S(1)} collective-permute-done((bf16[128,2048]{1,0:T(8,128)(2,1)S(1)}, bf16[128,2048]{1,0:T(8,128)(2,1)S(1)}, u32[]{:S(2)}, u32[]{:S(2)}) %collective-permute-start.17) | collective-permute-done | bytes 524320 | tf_op jit(solution)/shard_map/ppermute | solution.py:38
  178.0 2.6 copy.48
  182.9 2.8 slice-done.1
  187.3 11.3 %fusion.2 = f32[2,576,1536]{2,1,0:T(8,128)} fusion(bf16[2,576,2048]{2,1,0:T(8,128)(2,1)} %bitcast.198, bf16[2,2048,1536]{2,0,1:T(2,128)(2,1)S(1)} %bitcast.188), kind=kOutput, calls=%fused_computation.3 | convolution fusion | flops 7247757312 | bytes 24379392 | tf_op jit(solution)/shard_map/emd,edh->emh/dot_general | solution.py:129
  198.6 12.2 %multiply_reduce_fusion = (bf16[2,576]{1,0:T(2,128)(2,1)S(1)}, bf16[2,576,768]{2,1,0:T(8,128)(2,1)}, bf16[2,576,768]{2,1,0:T(8,128)(2,1)}, bf16[2,576,768]{2,1,0:T(8,128)(2,1)}) fusion(f32[2,576,1536]{2,1,0:T(8,128)} %fusion.2, bf16[2,576,2048]{2,1,0:T(8,128)(2,1)S(1)} %bitcast.189, bf16[2,2048,768]{2,0,1:T(2,128)(2,1)} %bitcast.210), kind=kOutput, calls=%fused_computation.20 | convolution fusion | flops 3639802880 | bytes 23398656 | tf_op jit(solution)/shard_map/emd,edh->emh/dot_general | solution.py:138
  210.8 13.1 %fusion.10 = bf16[2,576,2048]{2,1,0:T(8,128)(2,1)S(1)} fusion(bf16[2,2048,1536]{2,0,1:T(2,128)(2,1)} %pad_maximum_fusion, bf16[2,576,768]{2,1,0:T(8,128)(2,1)} %get-tuple-element.32, bf16[2,576,768]{2,1,0:T(8,128)(2,1)} %get-tuple-element.33), kind=kOutput, calls=%fused_computation.16 | convolution fusion | flops 7257194496 | bytes 20840448 | tf_op jit(solution)/shard_map/emh,edh->emd/dot_general | solution.py:148
  225.7 1.6 collective-permute-start.38
  227.8 1.7 fusion.16
  229.5 1.6 collective-permute-start.30
  231.2 1.7 fusion.17
  233.4 4.5 %convolution_convert_fusion = bf16[2,512,1536]{2,1,0:T(8,128)(2,1)S(1)} fusion(bf16[2,576,2048]{2,1,0:T(8,128)(2,1)} %bitcast.199, s32[]{:T(128)S(6)} %select_n.133, bf16[2,576,768]{2,1,0:T(8,128)(2,1)S(1)} %copy-done.9, bf16[2,576,768]{2,1,0:T(8,128)(2,1)S(1)} %copy-done.11), kind=kOutput, calls=%fused_computation.17 | convolution fusion | flops 1820590080 | bytes 7864324 | tf_op jit(solution)/shard_map/emd,emh->edh/dot_general | solution.py:71
  238.1 4.1 %convolution_convert_fusion.1 = bf16[2,512,1536]{2,1,0:T(8,128)(2,1)} fusion(bf16[2,576,2048]{2,1,0:T(8,128)(2,1)S(1)} %bitcast.203, s32[]{:T(128)S(6)} %select_n.131, bf16[2,576,768]{2,1,0:T(8,128)(2,1)S(1)} %copy-done.9, bf16[2,576,768]{2,1,0:T(8,128)(2,1)S(1)} %copy-done.11), kind=kOutput, calls=%fused_computation.18 | convolution fusion | flops 1820590080 | bytes 7864324 | tf_op jit(solution)/shard_map/emd,emh->edh/dot_general | solution.py:71
  244.3 1.7 collective-permute-start.40
  246.0 22.5 %collective-permute-done.31 = bf16[2,128,2048]{2,1,0:T(8,128)(2,1)S(1)} collective-permute-done((bf16[2,128,2048]{2,1,0:T(8,128)(2,1)S(1)}, bf16[2,128,2048]{2,1,0:T(8,128)(2,1)S(1)}, u32[]{:S(2)}, u32[]{:S(2)}) %collective-permute-start.31) | collective-permute-done | bytes 1048608 | tf_op jit(solution)/shard_map/ppermute | solution.py:49
  272.5 6.2 %collective-permute-done.32 = bf16[128,2048]{1,0:T(8,128)(2,1)S(1)} collective-permute-done((bf16[128,2048]{1,0:T(8,128)(2,1)S(1)}, bf16[128,2048]{1,0:T(8,128)(2,1)S(1)}, u32[]{:S(2)}, u32[]{:S(2)}) %collective-permute-start.32) | collective-permute-done | bytes 524320 | tf_op jit(solution)/shard_map/ppermute | solution.py:58
  278.7 4.4 %collective-permute-start.41 = (f32[8,128]{1,0:T(8,128)S(1)}, f32[8,128]{1,0:T(8,128)S(1)}, u32[]{:S(2)}, u32[]{:S(2)}) collective-permute-start(f32[8,128]{1,0:T(8,128)S(1)} %get-tuple-element.70), channel_id=1, source_target_pairs={{0,2},{1,3},{2,4},{3,5},{8,10},{9,11},{10,12},{11,13},{16,18},{17,... | collective-permute-start | bytes 12296 | tf_op jit(solution)/shard_map/ppermute | solution.py:58
  284.1 2.6 collective-permute-start.33
  286.7 6.1 %add_convert_fusion.1 = bf16[2,512,1536]{2,1,0:T(8,128)(2,1)} fusion(bf16[2,512,1536]{2,1,0:T(8,128)(2,1)S(1)} %collective-permute-done.47, bf16[2,576,2048]{2,1,0:T(8,128)(2,1)S(1)} %bitcast.204, s32[]{:T(128)S(6)} %select_n.132, bf16[2,576,768]{2,1,0:T(8,128)(2,1)S(1)} %copy-done.9, bf16[2,576,768]{2,1,0:T(8,128)(2,1)} %get-tuple-element.33), kind=kOutput, calls=%fused_computation.10 | convolution fusion | flops 1823735808 | bytes 11010052 | tf_op jit(solution)/shard_map/emd,emh->edh/dot_general | solution.py:71
  295.2 2.7 convolution_convert_fusion.3
  297.8 5.1 %collective-permute-start.42 = (f32[8,128]{1,0:T(8,128)S(1)}, f32[8,128]{1,0:T(8,128)S(1)}, u32[]{:S(2)}, u32[]{:S(2)}) collective-permute-start(f32[8,128]{1,0:T(8,128)S(1)} %get-tuple-element.68), channel_id=1, source_target_pairs={{0,2},{1,3},{2,4},{3,5},{4,6},{5,7},{8,10},{9,11},{10,12},{11,13},... | collective-permute-start | bytes 12296 | tf_op jit(solution)/shard_map/ppermute | solution.py:58
  305.4 6.0 %collective-permute-start.34 = (bf16[128,2048]{1,0:T(8,128)(2,1)}, bf16[128,2048]{1,0:T(8,128)(2,1)S(1)}, u32[]{:S(2)}, u32[]{:S(2)}) collective-permute-start(bf16[128,2048]{1,0:T(8,128)(2,1)} %get-tuple-element.44), channel_id=1, source_target_pairs={{0,2},{1,3},{2,4},{3,5},{4,6},{5,7},{8,10},{9,11},{10,12},{11,13},... | collective-permute-start | bytes 1572872 | tf_op jit(solution)/shard_map/ppermute | solution.py:58
  311.4 2.7 add_convert_fusion.3
  315.6 3.5 fusion.41
  320.5 4.0 fusion.49
  325.0 10.2 %collective-permute-done.37 = bf16[128,2048]{1,0:T(8,128)(2,1)S(1)} collective-permute-done((bf16[128,2048]{1,0:T(8,128)(2,1)S(1)}, bf16[128,2048]{1,0:T(8,128)(2,1)S(1)}, u32[]{:S(2)}, u32[]{:S(2)}) %collective-permute-start.37) | collective-permute-done | bytes 524320 | tf_op jit(solution)/shard_map/ppermute | solution.py:59
  336.3 51.4 %collective-permute-done.51 = bf16[2,512,768]{2,1,0:T(8,128)(2,1)} collective-permute-done((bf16[2,512,768]{2,1,0:T(8,128)(2,1)}, bf16[2,512,768]{2,1,0:T(8,128)(2,1)}, u32[]{:S(2)}, u32[]{:S(2)}) %collective-permute-start.51) | collective-permute-done | bytes 1572896 | tf_op jit(solution)/shard_map/ppermute | solution.py:77
  387.6 2.5 fusion.18
  390.2 4.2 %add_convert_fusion = bf16[2,512,1536]{2,1,0:T(8,128)(2,1)S(1)} fusion(bf16[2,512,1536]{2,1,0:T(8,128)(2,1)} %collective-permute-done.48, f32[2,512,1536]{2,1,0:T(8,128)S(1)} %fusion.49, bf16[2,512,1536]{2,1,0:T(8,128)(2,1)} %collective-permute-done.46), kind=kLoop, calls=%fused_computation.9 | loop fusion | flops 7864320 | bytes 15728640 | tf_op jit(solution)/shard_map/convert_element_type | solution.py:82
  394.6 2.4 maximum_bitcast_fusion
  397.0 9.4 %copy.60 = bf16[512,3,2,768]{3,2,1,0:T(2,128)(2,1)} copy(bf16[512,3,2,768]{3,0,2,1:T(8,128)(2,1)} %maximum_bitcast_fusion) | data formatting | bytes 9437184
  (180 shorter events, 60.4 us)
Async XLA Ops:
  2.7 32.1 %collective-permute-start.1 = (f32[16,128]{1,0:T(8,128)S(1)}, f32[16,128]{1,0:T(8,128)S(1)}, u32[]{:S(2)}, u32[]{:S(2)}) collective-permute-start(f32[16,128]{1,0:T(8,128)S(1)} %pad_maximum_fusion.2), channel_id=1, source_target_pairs={{2,0},{3,1},{4,2},{5,3},{6,4},{7,5},{10,8},{11,9},{12,10},{13,11},... | collective-permute-start | bytes 24584 | tf_op jit(solution)/shard_map/ppermute | solution.py:33
  4.0 32.1 %collective-permute-start = (f32[16,128]{1,0:T(8,128)S(1)}, f32[16,128]{1,0:T(8,128)S(1)}, u32[]{:S(2)}, u32[]{:S(2)}) collective-permute-start(f32[16,128]{1,0:T(8,128)S(1)} %pad_maximum_fusion.2), channel_id=1, source_target_pairs={{0,2},{1,3},{2,4},{3,5},{4,6},{5,7},{8,10},{9,11},{10,12},{11,13},... | collective-permute-start | bytes 24584 | tf_op jit(solution)/shard_map/ppermute | solution.py:32
  9.6 39.4 %collective-permute-start.6 = (f32[16,128]{1,0:T(8,128)S(1)}, f32[16,128]{1,0:T(8,128)S(1)}, u32[]{:S(2)}, u32[]{:S(2)}) collective-permute-start(f32[16,128]{1,0:T(8,128)S(1)} %pad_maximum_fusion.2), channel_id=1, source_target_pairs={{0,1},{1,0},{2,3},{3,2},{4,5},{5,4},{6,7},{7,6},{8,9},{9,8},{10,11... | collective-permute-start | bytes 24584 | tf_op jit(solution)/shard_map/ppermute | solution.py:38
  11.6 51.3 %collective-permute-start.20 = (bf16[128,2048]{1,0:T(8,128)(2,1)}, bf16[128,2048]{1,0:T(8,128)(2,1)S(1)}, u32[]{:S(2)}, u32[]{:S(2)}) collective-permute-start(bf16[128,2048]{1,0:T(8,128)(2,1)} %param.7), channel_id=1, source_target_pairs={{0,2},{1,3},{2,4},{3,5},{4,6},{5,7},{8,10},{9,11},{10,12},{11,13},... | collective-permute-start | bytes 1572872 | tf_op jit(solution)/shard_map/ppermute | solution.py:32
  15.1 108.4 %collective-permute-start.26 = (bf16[128,2048]{1,0:T(8,128)(2,1)}, bf16[128,2048]{1,0:T(8,128)(2,1)S(1)}, u32[]{:S(2)}, u32[]{:S(2)}) collective-permute-start(bf16[128,2048]{1,0:T(8,128)(2,1)} %param.7), channel_id=1, source_target_pairs={{0,1},{1,0},{2,3},{3,2},{4,5},{5,4},{6,7},{7,6},{8,9},{9,8},{10,11... | collective-permute-start | bytes 1572872 | tf_op jit(solution)/shard_map/ppermute | solution.py:38
  34.8 5.5 %collective-permute-start.2 = (f32[16,128]{1,0:T(8,128)S(1)}, f32[16,128]{1,0:T(8,128)S(1)}, u32[]{:S(2)}, u32[]{:S(2)}) collective-permute-start(f32[16,128]{1,0:T(8,128)S(1)} %collective-permute-done.1), channel_id=1, source_target_pairs={{2,0},{3,1},{4,2},{5,3},{10,8},{11,9},{12,10},{13,11},{18,16},{19,... | collective-permute-start | bytes 24584 | tf_op jit(solution)/shard_map/ppermute | solution.py:33
  36.2 5.6 %collective-permute-start.4 = (f32[16,128]{1,0:T(8,128)S(1)}, f32[16,128]{1,0:T(8,128)S(1)}, u32[]{:S(2)}, u32[]{:S(2)}) collective-permute-start(f32[16,128]{1,0:T(8,128)S(1)} %collective-permute-done), channel_id=1, source_target_pairs={{2,4},{3,5},{4,6},{5,7},{10,12},{11,13},{12,14},{13,15},{18,20},{1... | collective-permute-start | bytes 24584 | tf_op jit(solution)/shard_map/ppermute | solution.py:32
  40.4 5.7 %collective-permute-start.3 = (f32[16,128]{1,0:T(8,128)S(1)}, f32[16,128]{1,0:T(8,128)S(1)}, u32[]{:S(2)}, u32[]{:S(2)}) collective-permute-start(f32[16,128]{1,0:T(8,128)S(1)} %collective-permute-done.2), channel_id=1, source_target_pairs={{2,0},{3,1},{10,8},{11,9},{18,16},{19,17},{26,24},{27,25}} | collective-permute-start | bytes 24584 | tf_op jit(solution)/shard_map/ppermute | solution.py:33
  41.8 19.6 %collective-permute-start.21 = (bf16[128,2048]{1,0:T(8,128)(2,1)S(1)}, bf16[128,2048]{1,0:T(8,128)(2,1)S(1)}, u32[]{:S(2)}, u32[]{:S(2)}) collective-permute-start(bf16[128,2048]{1,0:T(8,128)(2,1)S(1)} %copy-done.4), channel_id=1, source_target_pairs={{2,0},{3,1},{4,2},{5,3},{6,4},{7,5},{10,8},{11,9},{12,10},{13,11},... | collective-permute-start | bytes 1572872 | tf_op jit(solution)/shard_map/ppermute | solution.py:33
  46.8 16.9 %collective-permute-start.10 = (bf16[128,2048]{1,0:T(8,128)(2,1)S(1)}, bf16[128,2048]{1,0:T(8,128)(2,1)S(1)}, u32[]{:S(2)}, u32[]{:S(2)}) collective-permute-start(bf16[128,2048]{1,0:T(8,128)(2,1)S(1)} %copy-done.5), channel_id=1, source_target_pairs={{0,2},{1,3},{2,4},{3,5},{4,6},{5,7},{8,10},{9,11},{10,12},{11,13},... | collective-permute-start | bytes 1572872 | tf_op jit(solution)/shard_map/ppermute | solution.py:32
  49.0 3.7 collective-permute-start.7
  60.0 20.8 %collective-permute-start.11 = (bf16[128,2048]{1,0:T(8,128)(2,1)S(1)}, bf16[128,2048]{1,0:T(8,128)(2,1)S(1)}, u32[]{:S(2)}, u32[]{:S(2)}) collective-permute-start(bf16[128,2048]{1,0:T(8,128)(2,1)S(1)} %copy-done.5), channel_id=1, source_target_pairs={{2,0},{3,1},{4,2},{5,3},{6,4},{7,5},{10,8},{11,9},{12,10},{13,11},... | collective-permute-start | bytes 1572872 | tf_op jit(solution)/shard_map/ppermute | solution.py:33
  61.3 30.7 %collective-permute-start.22 = (bf16[128,2048]{1,0:T(8,128)(2,1)S(1)}, bf16[128,2048]{1,0:T(8,128)(2,1)S(1)}, u32[]{:S(2)}, u32[]{:S(2)}) collective-permute-start(bf16[128,2048]{1,0:T(8,128)(2,1)S(1)} %collective-permute-done.21), channel_id=1, source_target_pairs={{2,0},{3,1},{4,2},{5,3},{10,8},{11,9},{12,10},{13,11},{18,16},{19,... | collective-permute-start | bytes 1572872 | tf_op jit(solution)/shard_map/ppermute | solution.py:33
  62.9 31.6 %collective-permute-start.24 = (bf16[128,2048]{1,0:T(8,128)(2,1)S(1)}, bf16[128,2048]{1,0:T(8,128)(2,1)S(1)}, u32[]{:S(2)}, u32[]{:S(2)}) collective-permute-start(bf16[128,2048]{1,0:T(8,128)(2,1)S(1)} %collective-permute-done.20), channel_id=1, source_target_pairs={{2,4},{3,5},{4,6},{5,7},{10,12},{11,13},{12,14},{13,15},{18,20},{1... | collective-permute-start | bytes 1572872 | tf_op jit(solution)/shard_map/ppermute | solution.py:32
  63.6 32.4 %collective-permute-start.14 = (bf16[128,2048]{1,0:T(8,128)(2,1)S(1)}, bf16[128,2048]{1,0:T(8,128)(2,1)S(1)}, u32[]{:S(2)}, u32[]{:S(2)}) collective-permute-start(bf16[128,2048]{1,0:T(8,128)(2,1)S(1)} %collective-permute-done.10), channel_id=1, source_target_pairs={{2,4},{3,5},{4,6},{5,7},{10,12},{11,13},{12,14},{13,15},{18,20},{1... | collective-permute-start | bytes 1572872 | tf_op jit(solution)/shard_map/ppermute | solution.py:32
  80.8 20.4 %collective-permute-start.12 = (bf16[128,2048]{1,0:T(8,128)(2,1)S(1)}, bf16[128,2048]{1,0:T(8,128)(2,1)S(1)}, u32[]{:S(2)}, u32[]{:S(2)}) collective-permute-start(bf16[128,2048]{1,0:T(8,128)(2,1)S(1)} %collective-permute-done.11), channel_id=1, source_target_pairs={{2,0},{3,1},{4,2},{5,3},{10,8},{11,9},{12,10},{13,11},{18,16},{19,... | collective-permute-start | bytes 1572872 | tf_op jit(solution)/shard_map/ppermute | solution.py:33
  92.0 17.8 %collective-permute-start.23 = (bf16[128,2048]{1,0:T(8,128)(2,1)S(1)}, bf16[128,2048]{1,0:T(8,128)(2,1)S(1)}, u32[]{:S(2)}, u32[]{:S(2)}) collective-permute-start(bf16[128,2048]{1,0:T(8,128)(2,1)S(1)} %collective-permute-done.22), channel_id=1, source_target_pairs={{2,0},{3,1},{10,8},{11,9},{18,16},{19,17},{26,24},{27,25}} | collective-permute-start | bytes 1572872 | tf_op jit(solution)/shard_map/ppermute | solution.py:33
  94.5 30.7 %collective-permute-start.16 = (bf16[128,2048]{1,0:T(8,128)(2,1)S(1)}, bf16[128,2048]{1,0:T(8,128)(2,1)S(1)}, u32[]{:S(2)}, u32[]{:S(2)}) collective-permute-start(bf16[128,2048]{1,0:T(8,128)(2,1)S(1)} %copy-done.5), channel_id=1, source_target_pairs={{0,1},{1,0},{2,3},{3,2},{4,5},{5,4},{6,7},{7,6},{8,9},{9,8},{10,11... | collective-permute-start | bytes 1572872 | tf_op jit(solution)/shard_map/ppermute | solution.py:38
  96.0 16.9 %collective-permute-start.25 = (bf16[128,2048]{1,0:T(8,128)(2,1)S(1)}, bf16[128,2048]{1,0:T(8,128)(2,1)S(1)}, u32[]{:S(2)}, u32[]{:S(2)}) collective-permute-start(bf16[128,2048]{1,0:T(8,128)(2,1)S(1)} %collective-permute-done.24), channel_id=1, source_target_pairs={{4,6},{5,7},{12,14},{13,15},{20,22},{21,23},{28,30},{29,31}} | collective-permute-start | bytes 1572872 | tf_op jit(solution)/shard_map/ppermute | solution.py:32
  101.2 21.6 %collective-permute-start.15 = (bf16[128,2048]{1,0:T(8,128)(2,1)S(1)}, bf16[128,2048]{1,0:T(8,128)(2,1)S(1)}, u32[]{:S(2)}, u32[]{:S(2)}) collective-permute-start(bf16[128,2048]{1,0:T(8,128)(2,1)S(1)} %collective-permute-done.14), channel_id=1, source_target_pairs={{4,6},{5,7},{12,14},{13,15},{20,22},{21,23},{28,30},{29,31}} | collective-permute-start | bytes 1572872 | tf_op jit(solution)/shard_map/ppermute | solution.py:32
  109.8 11.1 %collective-permute-start.13 = (bf16[128,2048]{1,0:T(8,128)(2,1)S(1)}, bf16[128,2048]{1,0:T(8,128)(2,1)S(1)}, u32[]{:S(2)}, u32[]{:S(2)}) collective-permute-start(bf16[128,2048]{1,0:T(8,128)(2,1)S(1)} %collective-permute-done.12), channel_id=1, source_target_pairs={{2,0},{3,1},{10,8},{11,9},{18,16},{19,17},{26,24},{27,25}} | collective-permute-start | bytes 1572872 | tf_op jit(solution)/shard_map/ppermute | solution.py:33
  113.9 39.0 %collective-permute-start.29 = (bf16[128,2048]{1,0:T(8,128)(2,1)S(1)}, bf16[128,2048]{1,0:T(8,128)(2,1)S(1)}, u32[]{:S(2)}, u32[]{:S(2)}) collective-permute-start(bf16[128,2048]{1,0:T(8,128)(2,1)S(1)} %get-tuple-element.15), channel_id=1, source_target_pairs={{0,1},{1,0},{2,3},{3,2},{4,5},{5,4},{6,7},{7,6},{8,9},{9,8},{10,11... | collective-permute-start | bytes 1572872 | tf_op jit(solution)/shard_map/ppermute | solution.py:38
  120.9 31.9 %collective-permute-start.28 = (bf16[128,2048]{1,0:T(8,128)(2,1)S(1)}, bf16[128,2048]{1,0:T(8,128)(2,1)S(1)}, u32[]{:S(2)}, u32[]{:S(2)}) collective-permute-start(bf16[128,2048]{1,0:T(8,128)(2,1)S(1)} %get-tuple-element.17), channel_id=1, source_target_pairs={{0,1},{1,0},{2,3},{3,2},{4,5},{5,4},{6,7},{7,6},{8,9},{9,8},{10,11... | collective-permute-start | bytes 1572872 | tf_op jit(solution)/shard_map/ppermute | solution.py:38
  122.8 28.4 %collective-permute-start.27 = (bf16[128,2048]{1,0:T(8,128)(2,1)S(1)}, bf16[128,2048]{1,0:T(8,128)(2,1)S(1)}, u32[]{:S(2)}, u32[]{:S(2)}) collective-permute-start(bf16[128,2048]{1,0:T(8,128)(2,1)S(1)} %get-tuple-element.19), channel_id=1, source_target_pairs={{0,1},{1,0},{2,3},{3,2},{4,5},{5,4},{6,7},{7,6},{8,9},{9,8},{10,11... | collective-permute-start | bytes 1572872 | tf_op jit(solution)/shard_map/ppermute | solution.py:38
  123.5 57.1 %collective-permute-start.19 = (bf16[128,2048]{1,0:T(8,128)(2,1)S(1)}, bf16[128,2048]{1,0:T(8,128)(2,1)S(1)}, u32[]{:S(2)}, u32[]{:S(2)}) collective-permute-start(bf16[128,2048]{1,0:T(8,128)(2,1)S(1)} %get-tuple-element.21), channel_id=1, source_target_pairs={{0,1},{1,0},{2,3},{3,2},{4,5},{5,4},{6,7},{7,6},{8,9},{9,8},{10,11... | collective-permute-start | bytes 1572872 | tf_op jit(solution)/shard_map/ppermute | solution.py:38
  125.2 55.4 %collective-permute-start.18 = (bf16[128,2048]{1,0:T(8,128)(2,1)S(1)}, bf16[128,2048]{1,0:T(8,128)(2,1)S(1)}, u32[]{:S(2)}, u32[]{:S(2)}) collective-permute-start(bf16[128,2048]{1,0:T(8,128)(2,1)S(1)} %get-tuple-element.23), channel_id=1, source_target_pairs={{0,1},{1,0},{2,3},{3,2},{4,5},{5,4},{6,7},{7,6},{8,9},{9,8},{10,11... | collective-permute-start | bytes 1572872 | tf_op jit(solution)/shard_map/ppermute | solution.py:38
  151.2 25.4 %collective-permute-start.17 = (bf16[128,2048]{1,0:T(8,128)(2,1)S(1)}, bf16[128,2048]{1,0:T(8,128)(2,1)S(1)}, u32[]{:S(2)}, u32[]{:S(2)}) collective-permute-start(bf16[128,2048]{1,0:T(8,128)(2,1)S(1)} %get-tuple-element.25), channel_id=1, source_target_pairs={{0,1},{1,0},{2,3},{3,2},{4,5},{5,4},{6,7},{7,6},{8,9},{9,8},{10,11... | collective-permute-start | bytes 1572872 | tf_op jit(solution)/shard_map/ppermute | solution.py:38
  225.7 18.5 %collective-permute-start.38 = (f32[2,8,128]{2,1,0:T(8,128)S(1)}, f32[2,8,128]{2,1,0:T(8,128)S(1)}, u32[]{:S(2)}, u32[]{:S(2)}) collective-permute-start(f32[2,8,128]{2,1,0:T(8,128)S(1)} %pad_maximum_fusion.3), channel_id=1, source_target_pairs={{0,1},{1,0},{2,3},{3,2},{4,5},{5,4},{6,7},{7,6},{8,9},{9,8},{10,11... | collective-permute-start | bytes 24584 | tf_op jit(solution)/shard_map/ppermute | solution.py:49
  227.3 16.4 %collective-permute-start.39 = (f32[2,8,128]{2,1,0:T(8,128)S(1)}, f32[2,8,128]{2,1,0:T(8,128)S(1)}, u32[]{:S(2)}, u32[]{:S(2)}) collective-permute-start(f32[2,8,128]{2,1,0:T(8,128)S(1)} %pad_maximum_fusion.4), channel_id=1, source_target_pairs={{0,1},{1,0},{2,3},{3,2},{4,5},{5,4},{6,7},{7,6},{8,9},{9,8},{10,11... | collective-permute-start | bytes 24584 | tf_op jit(solution)/shard_map/ppermute | solution.py:49
  229.5 42.4 %collective-permute-start.30 = (bf16[2,128,2048]{2,1,0:T(8,128)(2,1)S(1)}, bf16[2,128,2048]{2,1,0:T(8,128)(2,1)S(1)}, u32[]{:S(2)}, u32[]{:S(2)}) collective-permute-start(bf16[2,128,2048]{2,1,0:T(8,128)(2,1)S(1)} %fusion.16), channel_id=1, source_target_pairs={{0,1},{1,0},{2,3},{3,2},{4,5},{5,4},{6,7},{7,6},{8,9},{9,8},{10,11... | collective-permute-start | bytes 3145736 | tf_op jit(solution)/shard_map/ppermute | solution.py:49
  232.9 35.7 %collective-permute-start.31 = (bf16[2,128,2048]{2,1,0:T(8,128)(2,1)S(1)}, bf16[2,128,2048]{2,1,0:T(8,128)(2,1)S(1)}, u32[]{:S(2)}, u32[]{:S(2)}) collective-permute-start(bf16[2,128,2048]{2,1,0:T(8,128)(2,1)S(1)} %fusion.17), channel_id=1, source_target_pairs={{0,1},{1,0},{2,3},{3,2},{4,5},{5,4},{6,7},{7,6},{8,9},{9,8},{10,11... | collective-permute-start | bytes 3145736 | tf_op jit(solution)/shard_map/ppermute | solution.py:49
  238.0 46.1 %collective-permute-start.47 = (bf16[2,512,1536]{2,1,0:T(8,128)(2,1)S(1)}, bf16[2,512,1536]{2,1,0:T(8,128)(2,1)S(1)}, u32[]{:S(2)}, u32[]{:S(2)}) collective-permute-start(bf16[2,512,1536]{2,1,0:T(8,128)(2,1)S(1)} %convolution_convert_fusion), channel_id=1, source_target_pairs={{0,8},{8,0},{16,24},{24,16},{1,9},{9,1},{17,25},{25,17},{2,10},{10... | collective-permute-start | bytes 9437192 | tf_op jit(solution)/shard_map/ppermute | solution.py:74
  243.7 61.6 %collective-permute-start.50 = (bf16[2,512,768]{2,1,0:T(8,128)(2,1)S(1)}, bf16[2,512,768]{2,1,0:T(8,128)(2,1)S(1)}, u32[]{:S(2)}, u32[]{:S(2)}) collective-permute-start(bf16[2,512,768]{2,1,0:T(8,128)(2,1)S(1)} %convolution_convert_fusion.2), channel_id=1, source_target_pairs={{0,8},{8,0},{16,24},{24,16},{1,9},{9,1},{17,25},{25,17},{2,10},{10... | collective-permute-start | bytes 4718600 | tf_op jit(solution)/shard_map/ppermute | solution.py:74
  244.3 25.6 %collective-permute-start.40 = (f32[8,128]{1,0:T(8,128)S(1)}, f32[8,128]{1,0:T(8,128)S(1)}, u32[]{:S(2)}, u32[]{:S(2)}) collective-permute-start(f32[8,128]{1,0:T(8,128)S(1)} %get-tuple-element.72), channel_id=1, source_target_pairs={{0,2},{1,3},{8,10},{9,11},{16,18},{17,19},{24,26},{25,27}} | collective-permute-start | bytes 12296 | tf_op jit(solution)/shard_map/ppermute | solution.py:58
  269.8 8.9 %collective-permute-start.32 = (bf16[128,2048]{1,0:T(8,128)(2,1)S(1)}, bf16[128,2048]{1,0:T(8,128)(2,1)S(1)}, u32[]{:S(2)}, u32[]{:S(2)}) collective-permute-start(bf16[128,2048]{1,0:T(8,128)(2,1)S(1)} %get-tuple-element.48), channel_id=1, source_target_pairs={{0,2},{1,3},{8,10},{9,11},{16,18},{17,19},{24,26},{25,27}} | collective-permute-start | bytes 1572872 | tf_op jit(solution)/shard_map/ppermute | solution.py:58
  271.2 11.9 %collective-permute-start.35 = (bf16[128,2048]{1,0:T(8,128)(2,1)S(1)}, bf16[128,2048]{1,0:T(8,128)(2,1)S(1)}, u32[]{:S(2)}, u32[]{:S(2)}) collective-permute-start(bf16[128,2048]{1,0:T(8,128)(2,1)S(1)} %get-tuple-element.49), channel_id=1, source_target_pairs={{6,4},{7,5},{14,12},{15,13},{22,20},{23,21},{30,28},{31,29}} | collective-permute-start | bytes 1572872 | tf_op jit(solution)/shard_map/ppermute | solution.py:59
  271.9 118.2 %collective-permute-start.46 = (bf16[2,512,1536]{2,1,0:T(8,128)(2,1)}, bf16[2,512,1536]{2,1,0:T(8,128)(2,1)}, u32[]{:S(2)}, u32[]{:S(2)}) collective-permute-start(bf16[2,512,1536]{2,1,0:T(8,128)(2,1)} %convolution_convert_fusion.1), channel_id=1, source_target_pairs={{0,8},{8,0},{16,24},{24,16},{1,9},{9,1},{17,25},{25,17},{2,10},{10... | collective-permute-start | bytes 9437192 | tf_op jit(solution)/shard_map/ppermute | solution.py:74
  278.7 14.0 %collective-permute-start.41 = (f32[8,128]{1,0:T(8,128)S(1)}, f32[8,128]{1,0:T(8,128)S(1)}, u32[]{:S(2)}, u32[]{:S(2)}) collective-permute-start(f32[8,128]{1,0:T(8,128)S(1)} %get-tuple-element.70), channel_id=1, source_target_pairs={{0,2},{1,3},{2,4},{3,5},{8,10},{9,11},{10,12},{11,13},{16,18},{17,... | collective-permute-start | bytes 12296 | tf_op jit(solution)/shard_map/ppermute | solution.py:58
  283.1 10.5 %collective-permute-start.44 = (f32[8,128]{1,0:T(8,128)S(1)}, f32[8,128]{1,0:T(8,128)S(1)}, u32[]{:S(2)}, u32[]{:S(2)}) collective-permute-start(f32[8,128]{1,0:T(8,128)S(1)} %get-tuple-element.71), channel_id=1, source_target_pairs={{4,2},{5,3},{6,4},{7,5},{12,10},{13,11},{14,12},{15,13},{20,18},{2... | collective-permute-start | bytes 12296 | tf_op jit(solution)/shard_map/ppermute | solution.py:59
  284.1 13.8 %collective-permute-start.33 = (bf16[128,2048]{1,0:T(8,128)(2,1)S(1)}, bf16[128,2048]{1,0:T(8,128)(2,1)S(1)}, u32[]{:S(2)}, u32[]{:S(2)}) collective-permute-start(bf16[128,2048]{1,0:T(8,128)(2,1)S(1)} %get-tuple-element.46), channel_id=1, source_target_pairs={{0,2},{1,3},{2,4},{3,5},{8,10},{9,11},{10,12},{11,13},{16,18},{17,... | collective-permute-start | bytes 1572872 | tf_op jit(solution)/shard_map/ppermute | solution.py:58
  292.7 10.2 %collective-permute-start.36 = (bf16[128,2048]{1,0:T(8,128)(2,1)S(1)}, bf16[128,2048]{1,0:T(8,128)(2,1)S(1)}, u32[]{:S(2)}, u32[]{:S(2)}) collective-permute-start(bf16[128,2048]{1,0:T(8,128)(2,1)S(1)} %get-tuple-element.47), channel_id=1, source_target_pairs={{4,2},{5,3},{6,4},{7,5},{12,10},{13,11},{14,12},{15,13},{20,18},{2... | collective-permute-start | bytes 1572872 | tf_op jit(solution)/shard_map/ppermute | solution.py:59
  293.6 96.5 %collective-permute-start.48 = (bf16[2,512,1536]{2,1,0:T(8,128)(2,1)}, bf16[2,512,1536]{2,1,0:T(8,128)(2,1)}, u32[]{:S(2)}, u32[]{:S(2)}) collective-permute-start(bf16[2,512,1536]{2,1,0:T(8,128)(2,1)} %add_convert_fusion.1), channel_id=1, source_target_pairs={{0,16},{16,0},{8,24},{24,8},{1,17},{17,1},{9,25},{25,9},{2,18},{18... | collective-permute-start | bytes 9437192 | tf_op jit(solution)/shard_map/ppermute | solution.py:77
  297.8 16.2 %collective-permute-start.42 = (f32[8,128]{1,0:T(8,128)S(1)}, f32[8,128]{1,0:T(8,128)S(1)}, u32[]{:S(2)}, u32[]{:S(2)}) collective-permute-start(f32[8,128]{1,0:T(8,128)S(1)} %get-tuple-element.68), channel_id=1, source_target_pairs={{0,2},{1,3},{2,4},{3,5},{4,6},{5,7},{8,10},{9,11},{10,12},{11,13},... | collective-permute-start | bytes 12296 | tf_op jit(solution)/shard_map/ppermute | solution.py:58
  303.0 11.1 %collective-permute-start.45 = (f32[8,128]{1,0:T(8,128)S(1)}, f32[8,128]{1,0:T(8,128)S(1)}, u32[]{:S(2)}, u32[]{:S(2)}) collective-permute-start(f32[8,128]{1,0:T(8,128)S(1)} %get-tuple-element.69), channel_id=1, source_target_pairs={{2,0},{3,1},{4,2},{5,3},{6,4},{7,5},{10,8},{11,9},{12,10},{13,11},... | collective-permute-start | bytes 12296 | tf_op jit(solution)/shard_map/ppermute | solution.py:59
  305.4 13.7 %collective-permute-start.34 = (bf16[128,2048]{1,0:T(8,128)(2,1)}, bf16[128,2048]{1,0:T(8,128)(2,1)S(1)}, u32[]{:S(2)}, u32[]{:S(2)}) collective-permute-start(bf16[128,2048]{1,0:T(8,128)(2,1)} %get-tuple-element.44), channel_id=1, source_target_pairs={{0,2},{1,3},{2,4},{3,5},{4,6},{5,7},{8,10},{9,11},{10,12},{11,13},... | collective-permute-start | bytes 1572872 | tf_op jit(solution)/shard_map/ppermute | solution.py:58
  314.1 22.2 %collective-permute-start.49 = (bf16[2,512,768]{2,1,0:T(8,128)(2,1)}, bf16[2,512,768]{2,1,0:T(8,128)(2,1)}, u32[]{:S(2)}, u32[]{:S(2)}) collective-permute-start(bf16[2,512,768]{2,1,0:T(8,128)(2,1)} %convolution_convert_fusion.3), channel_id=1, source_target_pairs={{0,8},{8,0},{16,24},{24,16},{1,9},{9,1},{17,25},{25,17},{2,10},{10... | collective-permute-start | bytes 4718600 | tf_op jit(solution)/shard_map/ppermute | solution.py:74
  314.1 73.6 %collective-permute-start.51 = (bf16[2,512,768]{2,1,0:T(8,128)(2,1)}, bf16[2,512,768]{2,1,0:T(8,128)(2,1)}, u32[]{:S(2)}, u32[]{:S(2)}) collective-permute-start(bf16[2,512,768]{2,1,0:T(8,128)(2,1)} %add_convert_fusion.3), channel_id=1, source_target_pairs={{0,16},{16,0},{8,24},{24,8},{1,17},{17,1},{9,25},{25,9},{2,18},{18... | collective-permute-start | bytes 4718600 | tf_op jit(solution)/shard_map/ppermute | solution.py:77
  319.1 16.1 %collective-permute-start.37 = (bf16[128,2048]{1,0:T(8,128)(2,1)S(1)}, bf16[128,2048]{1,0:T(8,128)(2,1)S(1)}, u32[]{:S(2)}, u32[]{:S(2)}) collective-permute-start(bf16[128,2048]{1,0:T(8,128)(2,1)S(1)} %get-tuple-element.45), channel_id=1, source_target_pairs={{2,0},{3,1},{4,2},{5,3},{6,4},{7,5},{10,8},{11,9},{12,10},{13,11},... | collective-permute-start | bytes 1572872 | tf_op jit(solution)/shard_map/ppermute | solution.py:59
  (24 other events, 188.2 us)
